TPU v7x, 512 devices: a whole 4x8x8 slice. The times are simulated.
512 devices in a mesh: graph: 8 (over z), feat: 64 (over x, y, core).
Axes of the slice: x: 4, y: 8, z: 8, core: 2. Of those that a mesh axis runs over, the one named last changes fastest.
Arguments:
- features: bfloat16 [32768, 512], P('graph', 'feat'), may hold values from -6 to 6
- w_first: bfloat16 [2, 512, 256], P(None, 'feat'), may hold values from -0.25 to 0.25
- w_second: bfloat16 [2, 256, 256], replicated, may hold values from -0.375 to 0.375
- cotangent: bfloat16 [16384, 256], P(('graph', 'feat')), may hold values from -6 to 6
- nbr_first: int32 [16384, 15], P('graph'), may hold values from 0 to 4095
- send_rows: int32 [512, 8, 8], P(('graph', 'feat')), may hold values from -1 to 31, as said below
- nbr_second: int32 [16384, 10], P(('graph', 'feat')), may hold values from 0 to 95, as said below
Outputs:
- layer_out: bfloat16 [16384, 256], P(('graph', 'feat'))
- grad_second: float32 [2, 256, 256], replicated
- grad_first: float32 [2, 512, 256], P(None, 'feat')
Inputs may be any that keep to these rules, and one draw needn't show every extreme that they name: `send_rows`: for each device and partition the used slots come first; a device's own partition gets only -1; every used slot of a device to one partition names a different row; for each feat index some partition other than the last receives all 8 slots used from every other partition. `nbr_second`: each entry below 32 names an owned row; every other entry names a used slot received from another partition.
All inputs are finite; a program needn't handle non-finite values.
Results may differ from a plain program's by a relative error of at most 0.0051.
Values may be sent and summed in bfloat16 or wider, within the bound.
A program may use at most 64 MiB of HBM per device.

v0:
```python
import jax
import jax.numpy as jnp
from jax import lax
from jax.sharding import PartitionSpec as P

HID = 256
FAN1 = 15
FAN2 = 10
OWN = 32


def silu_grad(value):
    sig = jax.nn.sigmoid(value)
    return sig * (1.0 + value * (1.0 - sig))


def body(features, w_first, w_second, cotangent, nbr_first, send_rows, nbr_second):
    high = lax.Precision.HIGHEST
    targets = nbr_first.shape[0]
    gathered = features[nbr_first].astype(jnp.float32)
    mean_all = (jnp.sum(gathered, axis=1) / FAN1).astype(jnp.bfloat16)
    self_all = features[:targets]
    self_part = self_all
    mean_part = mean_all
    term = jnp.dot(self_part, w_first[0], preferred_element_type=jnp.float32)
    pre_one = lax.psum_scatter(
        term + jnp.dot(mean_part, w_first[1], preferred_element_type=jnp.float32),
        "feat",
        scatter_dimension=0,
        tiled=True,
    )
    hidden = jax.nn.silu(pre_one).astype(jnp.bfloat16)
    slot_rows = send_rows[0]
    valid = (slot_rows >= 0)[..., None]
    picked = hidden[jnp.maximum(slot_rows, 0)]
    outgoing_rows = jnp.where(valid, picked, jnp.zeros_like(picked))
    received = lax.all_to_all(outgoing_rows, "graph", split_axis=0, concat_axis=0, tiled=True)
    ext = jnp.concatenate([hidden, received.reshape(-1, HID)], axis=0)
    width = ext.shape[0]
    counts = jnp.zeros((OWN, width), jnp.float32)
    for k in range(FAN2):
        counts = counts + (nbr_second[:, k, None] == jnp.arange(width)[None, :]).astype(jnp.float32)
    mean_two = (
        jnp.dot(counts.astype(jnp.bfloat16), ext, preferred_element_type=jnp.float32) / FAN2
    ).astype(jnp.bfloat16)
    layer_out = jnp.dot(hidden, w_second[0], preferred_element_type=jnp.float32)
    layer_out = (
        layer_out + jnp.dot(mean_two, w_second[1], preferred_element_type=jnp.float32)
    ).astype(jnp.bfloat16)
    grad_terms = jnp.stack(
        [
            jnp.einsum("rh,ro->ho", hidden, cotangent, preferred_element_type=jnp.float32),
            jnp.einsum("rh,ro->ho", mean_two, cotangent, preferred_element_type=jnp.float32),
        ]
    )
    grad_second = lax.psum(grad_terms, ("graph", "feat"))
    d_self = jnp.einsum("ro,ho->rh", cotangent, w_second[0], preferred_element_type=jnp.float32)
    d_mean = (
        jnp.einsum("ro,ho->rh", cotangent, w_second[1], preferred_element_type=jnp.float32) / FAN2
    )
    d_ext = jnp.dot(counts.T, d_mean, precision=high)
    halo_grad = d_ext[OWN:].reshape(-1, slot_rows.shape[1], HID).astype(jnp.bfloat16)
    returned = lax.all_to_all(halo_grad, "graph", split_axis=0, concat_axis=0, tiled=True)
    onehot = (slot_rows.reshape(-1)[:, None] == jnp.arange(OWN)[None, :]).astype(jnp.bfloat16)
    d_back = jnp.einsum(
        "sr,sh->rh", onehot, returned.reshape(-1, HID), preferred_element_type=jnp.float32
    )
    d_hidden = d_self + d_ext[:OWN] + d_back
    d_pre = (d_hidden * silu_grad(pre_one)).astype(jnp.bfloat16)
    piece = lax.all_gather(d_pre, "feat", axis=0, tiled=True)
    self_part = self_all
    mean_part = mean_all
    first_sum = jnp.einsum("rf,rh->fh", self_part, piece, preferred_element_type=jnp.float32)
    second_sum = jnp.einsum("rf,rh->fh", mean_part, piece, preferred_element_type=jnp.float32)
    local_grad = jnp.stack([first_sum, second_sum])
    grad_first = lax.psum(local_grad, "graph")
    return (layer_out, grad_second, grad_first)


def solution(mesh):
    in_specs = (
        P("graph", "feat"),
        P(None, "feat", None),
        P(),
        P(("graph", "feat"), None),
        P("graph", None),
        P(("graph", "feat"), None, None),
        P(("graph", "feat"), None),
    )
    out_specs = (P(("graph", "feat"), None), P(), P(None, "feat", None))
    return jax.shard_map(body, mesh=mesh, in_specs=in_specs, out_specs=out_specs, check_vma=False)
```

profile of v0, /device:TPU:1, one launch (start us, length us, event | category | flops | bytes accessed | tf_op | source)
XLA Modules:
  0.0 665.3 jit_solution(17936867088784072761)
XLA Ops:
  7.2 0.9 compare_select_fusion
  8.2 0.4 copy.17
  8.5 0.6 reshape.38
  9.2 0.5 copy.18
  9.6 107.8 %gather_fusion = bf16[30720,8]{1,0:T(8,128)(2,1)} fusion(bf16[4096,8]{1,0:T(8,128)(2,1)S(1)} %copy.18, s32[30720]{0:T(1024)S(1)} %broadcast_clamp_fusion), kind=kCustom, calls=%fused_computation | custom fusion | bytes 1105920 | tf_op jit(solution)/shard_map/gather | solution.py:20
  117.4 5.7 copy.19
  123.1 12.7 %reshape.56 = f32[2048,15,8]{1,0,2:T(8,128)} reshape(bf16[30720,8]{0,1:T(8,128)(2,1)S(1)} %copy.19) | data formatting | bytes 1474560 | tf_op jit(solution)/shard_map/convert_element_type | solution.py:20
  135.8 0.5 fusion.19
  136.3 5.6 reduce_sum.9
  141.9 1.8 convolution_add_fusion
  143.8 0.7 copy-done.5
  144.4 0.3 copy-done.1
  144.8 0.4 fusion.23
  145.3 0.6 fusion.16
  145.9 10.9 %all-to-all-start.1 = ((bf16[8,8,256]{2,1,0:T(8,128)(2,1)}), bf16[8,8,256]{2,1,0:T(8,128)(2,1)S(1)}, u32[]{:S(2)}, u32[]{:S(2)}) async-start(bf16[8,8,256]{2,1,0:T(8,128)(2,1)} %fusion.16), calls=%async_computation.2 | async-start | bytes 65536 | tf_op jit(solution)/shard_map/all_to_all | solution.py:63
  157.1 6.6 all-to-all-done.1
  163.7 129.3 %reduce-scatter.2.cloned.1.call-done = f32[32,256]{1,0:T(8,128)} async-done(((f32[2048,256]{1,0:T(8,128)}), f32[32,256]{1,0:T(8,128)}) %reduce-scatter.2.cloned.1.call-update) | async-done | bytes 32784 | tf_op jit(solution)/shard_map/reduce_scatter | solution.py:26
  293.0 1.6 fusion.3
  294.7 0.8 multiply_convert_fusion.1
  295.5 0.7 gather_fusion.1
  296.2 0.7 bitcast_select_fusion
  296.9 7.1 %all-to-all-start = ((bf16[8,8,256]{2,1,0:T(8,128)(2,1)}), bf16[8,8,256]{2,1,0:T(8,128)(2,1)S(1)}, u32[]{:S(2)}, u32[]{:S(2)}) async-start(bf16[8,8,256]{2,1,0:T(8,128)(2,1)} %bitcast_select_fusion), calls=%async_computation.1 | async-start | bytes 65536 | tf_op jit(solution)/shard_map/all_to_all | solution.py:37
  304.5 6.5 all-to-all-done
  310.9 0.2 fusion.1
  311.4 0.8 pad_maximum_fusion
  312.2 0.8 fusion.2
  313.0 70.2 %all-gather.2.cloned.1.call-done = bf16[2048,256]{1,0:T(8,128)(2,1)} async-done(((bf16[32,256]{1,0:T(8,128)(2,1)}), bf16[2048,256]{1,0:T(8,128)(2,1)}) %all-gather.2.cloned.1.call-update) | async-done | bytes 1048592 | tf_op jit(solution)/shard_map/all_gather | solution.py:70
  383.2 1.5 convolution_bitcast_fusion.2
  384.7 1.5 convolution_bitcast_fusion.3
  386.2 24.3 %psum.15 = f32[2,8,256]{2,1,0:T(8,128)} all-reduce(f32[2,8,256]{2,1,0:T(8,128)S(1)} %pad_maximum_fusion.1), channel_id=1, replica_groups=mesh['graph'=8,'feat'=64] {'graph'}, use_global_device_ids=true, to_apply=%region_3.4 | all-reduce | flops 4096 | bytes 32768 | tf_op jit(solution)/shard_map/psum | solution.py:76
  410.4 246.5 %all-reduce.2.cloned.1.call-done = f32[2,256,256]{2,1,0:T(8,128)} async-done(((f32[2,256,256]{2,1,0:T(8,128)}), f32[2,256,256]{2,1,0:T(8,128)}) %all-reduce.2.cloned.1.call-update) | async-done | bytes 524304 | tf_op jit(solution)/shard_map/psum | solution.py:56
  656.9 1.9 copy.21
  (29 shorter events, 1.3 us)
Async XLA Ops:
  7.2 137.3 %copy-start = (bf16[32,256]{1,0:T(8,128)(2,1)S(1)}, bf16[32,256]{1,0:T(8,128)(2,1)}, u32[]{:S(2)}) copy-start(bf16[32,256]{1,0:T(8,128)(2,1)} %param.10) | copy-start | bytes 49156
  7.2 2.0 copy-start.2
  7.2 285.8 %reduce-scatter.2.cloned.1.call-start = ((), (), s32[]{:S(2)}) async-start(), calls=%async_computation.3 | async-start | bytes 2129920 | tf_op jit(solution)/shard_map/reduce_scatter | solution.py:26
  123.1 12.7 %copy-start.4 = (bf16[2,8,256]{2,1,0:T(8,128)(2,1)S(1)}, bf16[2,8,256]{2,1,0:T(8,128)(2,1)}, u32[]{:S(2)}) copy-start(bf16[2,8,256]{2,1,0:T(8,128)(2,1)} %param.8) | copy-start | bytes 24580
  143.7 0.7 copy-start.5
  143.7 1.0 copy-start.1
  143.7 13.2 %copy-start.3 = (s32[1,8,8]{2,1,0:T(8,128)S(1)}, s32[1,8,8]{2,1,0:T(8,128)}, u32[]{:S(2)}) copy-start(s32[1,8,8]{2,1,0:T(8,128)} %param.12) | copy-start | bytes 772
  145.9 17.7 %all-to-all-start.1 = ((bf16[8,8,256]{2,1,0:T(8,128)(2,1)}), bf16[8,8,256]{2,1,0:T(8,128)(2,1)S(1)}, u32[]{:S(2)}, u32[]{:S(2)}) async-start(bf16[8,8,256]{2,1,0:T(8,128)(2,1)} %fusion.16), calls=%async_computation.2 | async-start | bytes 65536 | tf_op jit(solution)/shard_map/all_to_all | solution.py:63
  156.8 226.5 %all-gather.2.cloned.1.call-start = ((), (), s32[]{:S(2)}) async-start(), calls=%async_computation.5 | async-start | bytes 1064960 | tf_op jit(solution)/shard_map/all_gather | solution.py:70
  296.9 14.0 %all-to-all-start = ((bf16[8,8,256]{2,1,0:T(8,128)(2,1)}), bf16[8,8,256]{2,1,0:T(8,128)(2,1)S(1)}, u32[]{:S(2)}, u32[]{:S(2)}) async-start(bf16[8,8,256]{2,1,0:T(8,128)(2,1)} %bitcast_select_fusion), calls=%async_computation.1 | async-start | bytes 65536 | tf_op jit(solution)/shard_map/all_to_all | solution.py:37
  304.1 352.8 %all-reduce.2.cloned.1.call-start = ((), (), s32[]{:S(2)}) async-start(), calls=%async_computation.4 | async-start | bytes 1048576 | tf_op jit(solution)/shard_map/psum | solution.py:56
Sparse Core Ops, SparseCore 0:
  143.9 149.0 reduce-scatter.1
  297.4 85.7 all-gather.1
  389.6 267.2 all-reduce.1
where the time goes:
time: 666 us; the launch traced here: 665 us
  waiting for transfers between devices  459 us (69%)
  local copies, waits for them, and re-layouts  132 us (20%)
  blocking collectives  24.3 us (4%)
  starting transfers between devices  18.1 us (3%)
  between operations  13.9 us (2%)
  matrix products  9.15 us (1%)
  other arithmetic  8.88 us (1%)
    psum x1, waiting for transfers between devices, body(): grad_second = lax.psum(grad_terms, ('graph', 'feat'))  246 us
    reduce_scatter x1, waiting for transfers between devices, body(): lax.psum_scatter(term + jnp.dot(mean_part, w_first[1], preferred_element_...  129 us
    gather x2, local copies, waits for them, and re-layouts, body(): gathered = features[nbr_first].astype(jnp.float32)  113 us
    all_gather x1, waiting for transfers between devices, body(): piece = lax.all_gather(d_pre, 'feat', axis=0, tiled=True)  70.2 us
    psum x1, blocking collectives, body(): grad_first = lax.psum(local_grad, 'graph')  24.3 us
  transfers between devices with their start and end apart: 5, of which 5 were waited for; matrix products, arithmetic and copies ran while one was open for 1% of the time, Pallas kernels for 0%

commit v1 on v0

v1 whole, which is shorter than its diff:
```python
import functools

import jax
import jax.numpy as jnp
from jax import lax
from jax.experimental import pallas as pl
from jax.experimental.pallas import tpu as pltpu
from jax.sharding import PartitionSpec as P

HID = 256
FAN1 = 15
FAN2 = 10
OWN = 32
HALO = 8
SRC = 4096
LO = 256
GROUPS = SRC // LO
BF16 = jnp.bfloat16
F32 = jnp.float32
MESH = pl.DeviceIdType.MESH


def select_tree(values, masks):
    for mask in masks:
        values = [
            jnp.where(mask, values[2 * i + 1], values[2 * i]) for i in range(len(values) // 2)
        ]
    return values[0]


def dot(a, b):
    return jnp.dot(a, b, preferred_element_type=F32)


def dot_lhs_t(a, b):
    return lax.dot_general(a, b, (((0,), (0,)), ((), ())), preferred_element_type=F32)


def dot_rhs_t(a, b):
    return lax.dot_general(a, b, (((1,), (1,)), ((), ())), preferred_element_type=F32)


def split(a):
    high = a.astype(BF16)
    return high, (a - high.astype(F32)).astype(BF16)


def kernel(
    n_graph, n_feat,
    feat_ref, w1_ref, w2_ref, cot_ref, near1_ref, send_ref, near2_ref,
    out_ref, g2_ref, g1_ref,
    table, x_own, x_all, w_all, pre_part, pre_in, d_all, hid_own, hid_in,
    v_out, v_in, e_out, e_in, hh_out, hh_in,
    gs_out, gs_in, gz, gz_in, gfin, gsib, dw_out, dw_in, dz, dz_in,
    send_sem, recv_sem,
):
    n_chip = n_feat // 2
    n_row = n_feat // 4
    targets = n_feat * OWN
    tile = min(512, targets)
    per_tile = tile // 128
    shard = HID // n_chip
    g = lax.axis_index("graph")
    f = lax.axis_index("feat")
    row, part = f // 4, f % 4
    chip, core = f // 2, f % 2
    sibling = f + 1 - 2 * core

    def remote(index, src, dst, graph, feat):
        return pltpu.make_async_remote_copy(
            src_ref=src, dst_ref=dst, send_sem=send_sem.at[index], recv_sem=recv_sem.at[index],
            device_id=(graph, feat), device_id_type=MESH,
        )

    def wait_in(index, ref):
        remote(index, ref, ref, g, sibling).wait_recv()

    def wait_out(index, ref):
        remote(index, ref, ref, g, sibling).wait_send()

    def loop(low, high, step):
        def body(i, carry):
            step(i)
            return carry

        lax.fori_loop(low, high, body, 0)

    barrier = pltpu.get_barrier_semaphore()

    def greet(graph, feat):
        pl.semaphore_signal(barrier, inc=1, device_id=(graph, feat), device_id_type=MESH)

    loop(1, n_chip, lambda j: greet(g, 2 * ((chip + j) % n_chip) + core))
    loop(1, n_graph, lambda j: greet((g + j) % n_graph, f))
    greet(g, sibling)
    greet(g, 4 * row + 3 - part)

    width = OWN + n_graph * HALO
    near2 = near2_ref[...]
    slots = lax.broadcasted_iota(jnp.int32, (width, OWN), 0)
    counts_t = jnp.zeros((width, OWN), F32)
    for k in range(FAN2):
        counts_t = counts_t + jnp.where(slots == near2[k : k + 1], 1.0, 0.0)
    counts_t = counts_t.astype(BF16)
    cot = cot_ref[...]
    e_all = dot(counts_t, cot)
    e_out[...] = e_all[OWN:].reshape(n_graph, HALO, HID)

    for s in range(GROUPS):
        table[s * 8 : (s + 1) * 8, :] = feat_ref[:, s * LO : (s + 1) * LO].astype(F32)
    lows = lax.broadcasted_iota(jnp.int32, (LO, tile), 0).astype(F32).astype(BF16)

    def gather(t):
        columns = pl.ds(pl.multiple_of(t * tile, tile), tile)
        near = near1_ref[:, columns]
        groups = table[...].astype(BF16)
        total = jnp.zeros((8, tile), F32)
        for k in range(FAN1):
            index = near[k : k + 1]
            low = jnp.broadcast_to((index % LO).astype(F32), (16, tile)).astype(BF16)
            low = jnp.concatenate([low] * (LO // 16), axis=0)
            picked = dot(groups, jnp.where(lows == low, jnp.ones((), BF16), jnp.zeros((), BF16)))
            high = jnp.broadcast_to(index // LO, (8, tile))
            masks = [(high // (1 << bit)) % 2 != 0 for bit in range(4)]
            total = total + select_tree([picked[s * 8 : (s + 1) * 8] for s in range(GROUPS)], masks)
        both = jnp.concatenate([feat_ref[:, columns].astype(F32), total / FAN1], axis=0).astype(BF16)
        for i in range(per_tile):
            block = t * per_tile + i
            x_own[block] = both[:, i * 128 : (i + 1) * 128]

    def send_x(t):
        for i in range(per_tile):
            block = t * per_tile + i

            @pl.when(block != row)
            def _():
                remote(1, x_own.at[block], x_all.at[(block - row + n_row) % n_row], g, 4 * block + part).start()

    n_tiles = targets // tile
    early = n_tiles // 2
    loop(0, early, gather)
    pl.semaphore_wait(barrier, n_chip - 1 + n_graph - 1 + 2)
    loop(1, n_row, lambda j: remote(0, w1_ref, w_all.at[j], g, 4 * ((row + j) % n_row) + part).start())
    loop(1, n_graph, lambda j: remote(2, e_out.at[(g + j) % n_graph], e_in.at[g], (g + j) % n_graph, f).start())
    loop(0, early, send_x)

    def gather_send(t):
        gather(t)
        send_x(t)

    loop(early, n_tiles, gather_send)
    w_all[0] = w1_ref[...]
    x_all[0] = x_own[row]

    rows = lax.broadcasted_iota(jnp.int32, (OWN, n_graph * HALO), 0)
    pick_t = jnp.where(rows == send_ref[...], 1.0, 0.0).astype(BF16)
    e_in[g] = jnp.zeros((HALO, HID), F32)
    wait_in(2, e_in.at[pl.ds(0, n_graph - 1)])
    back = e_in[...].reshape(n_graph * HALO, HID)
    back_high, back_low = split(back)
    e_total = (e_all[:OWN] + (dot(pick_t, back_high) + dot(pick_t, back_low))) / FAN2
    e_high, e_low = split(e_total)
    first = jnp.broadcast_to(core, (OWN, HID)) == 0
    cot32, e32 = cot.astype(F32), e_high.astype(F32)
    v_own = jnp.where(first, cot32, e32).astype(BF16)
    v_out[...] = jnp.where(first, e32, cot32).astype(BF16)
    remote(3, v_out, v_in, g, sibling).start()
    d_hidden = dot_rhs_t(cot, w2_ref[0]) + (dot_rhs_t(e_high, w2_ref[1]) + dot_rhs_t(e_low, w2_ref[1]))

    wait_in(0, w_all.at[pl.ds(1, n_row - 1)])
    wait_in(1, x_all.at[pl.ds(1, n_row - 1)])
    x = x_all[...].reshape(n_row * 16, 128)
    pre_part[...] = dot_lhs_t(x, w_all[...].reshape(n_row * 16, HID)).reshape(4, OWN, HID)
    for d in (1, 2, 3):
        remote(4, pre_part.at[(part + d) % 4], pre_in.at[d], g, 4 * row + (part + d) % 4).start()
    wait_in(4, pre_in.at[pl.ds(1, 3)])
    pre = (pre_part[part] + pre_in[1]) + (pre_in[2] + pre_in[3])
    sig = 1.0 / (1.0 + jnp.exp(-pre))
    hidden = (pre * sig).astype(BF16)
    hid_own[...] = hidden
    remote(5, hid_own, hid_in, g, sibling).start()
    d_all[part] = (d_hidden * (sig * (1.0 + pre * (1.0 - sig)))).astype(BF16)
    for d in (1, 2, 3):
        remote(6, d_all.at[part], d_all.at[part], g, 4 * row + (part + d) % 4).start()
    hh_out[...] = dot_lhs_t(pick_t, hidden).reshape(n_graph, HALO, HID)
    loop(1, n_graph, lambda j: remote(7, hh_out.at[(g + j) % n_graph], hh_in.at[g], (g + j) % n_graph, f).start())

    wait_in(3, v_in)
    v_pair = jnp.concatenate([v_own, v_in[...]], axis=0)
    wait_in(5, hid_in)
    grad = dot_lhs_t(jnp.concatenate([hidden, hid_in[...]], axis=0), v_pair).reshape(n_chip, shard, HID)
    gs_out[...] = jnp.concatenate([grad[:, :, :128], grad[:, :, 128:]], axis=1).astype(BF16)

    def send_grad(j):
        peer = (chip + j) % n_chip
        remote(8, gs_out.at[peer], gs_in.at[j], g, 2 * peer + core).start()

    loop(1, n_chip, send_grad)

    wait_in(6, d_all.at[pl.ds(0, 3)])
    dw_out[...] = dot(x, d_all[...].reshape(4 * OWN, HID)).reshape(n_row, 16, HID).astype(BF16)
    loop(1, n_row, lambda j: remote(9, dw_out.at[j], dw_in.at[j], g, 4 * ((row - j + n_row) % n_row) + part).start())

    gs_in[0] = gs_out[chip]
    wait_in(8, gs_in.at[pl.ds(1, n_chip - 1)])
    gz[...] = jnp.sum(gs_in[...].astype(F32), axis=0)
    gz_in[g] = gz[...]
    loop(1, n_graph, lambda j: remote(10, gz, gz_in.at[g], (g + j) % n_graph, f).start())

    hh_in[g] = jnp.zeros((HALO, HID), F32)
    wait_in(7, hh_in.at[pl.ds(0, n_graph - 1)])
    ext = jnp.concatenate([hidden.astype(F32), hh_in[...].reshape(n_graph * HALO, HID)], axis=0).astype(BF16)
    mean2 = (dot_lhs_t(counts_t, ext) / FAN2).astype(BF16)
    out_ref[...] = (dot(hidden, w2_ref[0]) + dot(mean2, w2_ref[1])).astype(BF16)

    wait_in(10, gz_in.at[pl.ds(0, n_graph - 1)])
    gfin[chip] = jnp.sum(gz_in[...], axis=0).astype(BF16)
    loop(1, n_chip, lambda j: remote(11, gfin.at[chip], gfin.at[chip], g, 2 * ((chip + j) % n_chip) + core).start())

    dw_in[0] = dw_out[0]
    wait_in(9, dw_in.at[pl.ds(1, n_row - 1)])
    dz[...] = jnp.sum(dw_in[...].astype(F32), axis=0)
    dz_in[g] = dz[...]
    loop(1, n_graph, lambda j: remote(12, dz, dz_in.at[g], (g + j) % n_graph, f).start())
    wait_in(12, dz_in.at[pl.ds(0, n_graph - 1)])
    g1_ref[...] = jnp.sum(dz_in[...], axis=0).reshape(2, 8, HID)

    def unpack(ref, which):
        both = ref[...].astype(F32)
        g2_ref[which, :, 0:128] = both[:, :shard].reshape(HID, 128)
        g2_ref[which, :, 128:256] = both[:, shard:].reshape(HID, 128)

    wait_in(11, gfin.at[pl.ds(0, n_chip - 1)])
    remote(13, gfin, gsib, g, sibling).start()
    unpack(gfin, core)
    wait_in(13, gsib)
    unpack(gsib, 1 - core)

    wait_out(0, w_all.at[pl.ds(1, n_row - 1)])
    wait_out(1, x_all.at[pl.ds(1, n_row - 1)])
    wait_out(2, e_in.at[pl.ds(0, n_graph - 1)])
    wait_out(3, v_in)
    wait_out(4, pre_in.at[pl.ds(1, 3)])
    wait_out(5, hid_in)
    wait_out(6, d_all.at[pl.ds(0, 3)])
    wait_out(7, hh_in.at[pl.ds(0, n_graph - 1)])
    wait_out(8, gs_in.at[pl.ds(1, n_chip - 1)])
    wait_out(9, dw_in.at[pl.ds(1, n_row - 1)])
    wait_out(10, gz_in.at[pl.ds(0, n_graph - 1)])
    wait_out(11, gfin.at[pl.ds(0, n_chip - 1)])
    wait_out(12, dz_in.at[pl.ds(0, n_graph - 1)])
    wait_out(13, gsib)


def solution(mesh):
    n_graph, n_feat = mesh.shape["graph"], mesh.shape["feat"]
    n_chip, n_row = n_feat // 2, n_feat // 4
    pack = 2 * HID // n_chip

    def body(features, w_first, w_second, cotangent, nbr_first, send_rows, nbr_second):
        vmem = pl.BlockSpec(memory_space=pltpu.VMEM)
        return pl.pallas_call(
            functools.partial(kernel, n_graph, n_feat),
            out_shape=(
                jax.ShapeDtypeStruct((OWN, HID), BF16),
                jax.ShapeDtypeStruct((2, HID, HID), F32),
                jax.ShapeDtypeStruct((2, 8, HID), F32),
            ),
            in_specs=[vmem] * 7,
            out_specs=(vmem,) * 3,
            scratch_shapes=[
                pltpu.VMEM((GROUPS * 8, LO), F32),
                pltpu.VMEM((n_row, 16, 128), BF16),
                pltpu.VMEM((n_row, 16, 128), BF16),
                pltpu.VMEM((n_row, 16, HID), BF16),
                pltpu.VMEM((4, OWN, HID), F32),
                pltpu.VMEM((4, OWN, HID), F32),
                pltpu.VMEM((4, OWN, HID), BF16),
                pltpu.VMEM((OWN, HID), BF16),
                pltpu.VMEM((OWN, HID), BF16),
                pltpu.VMEM((OWN, HID), BF16),
                pltpu.VMEM((OWN, HID), BF16),
                pltpu.VMEM((n_graph, HALO, HID), F32),
                pltpu.VMEM((n_graph, HALO, HID), F32),
                pltpu.VMEM((n_graph, HALO, HID), F32),
                pltpu.VMEM((n_graph, HALO, HID), F32),
                pltpu.VMEM((n_chip, pack, 128), BF16),
                pltpu.VMEM((n_chip, pack, 128), BF16),
                pltpu.VMEM((pack, 128), F32),
                pltpu.VMEM((n_graph, pack, 128), F32),
                pltpu.VMEM((n_chip, pack, 128), BF16),
                pltpu.VMEM((n_chip, pack, 128), BF16),
                pltpu.VMEM((n_row, 16, HID), BF16),
                pltpu.VMEM((n_row, 16, HID), BF16),
                pltpu.VMEM((16, HID), F32),
                pltpu.VMEM((n_graph, 16, HID), F32),
                pltpu.SemaphoreType.DMA((14,)),
                pltpu.SemaphoreType.DMA((14,)),
            ],
            compiler_params=pltpu.CompilerParams(
                collective_id=0, has_side_effects=True, vmem_limit_bytes=40 * 1024 * 1024
            ),
        )(
            features.T,
            w_first.reshape(16, HID),
            w_second,
            cotangent,
            nbr_first.T,
            send_rows.reshape(1, n_graph * HALO),
            nbr_second.T,
        )

    in_specs = (
        P("graph", "feat"),
        P(None, "feat", None),
        P(),
        P(("graph", "feat"), None),
        P("graph", None),
        P(("graph", "feat"), None, None),
        P(("graph", "feat"), None),
    )
    out_specs = (P(("graph", "feat"), None), P(), P(None, "feat", None))
    return jax.shard_map(body, mesh=mesh, in_specs=in_specs, out_specs=out_specs, check_vma=False)
```

time: 666 us -> 57.9 us (0.09)
  waiting for transfers between devices: 459 us -> 0 us
  local copies, waits for them, and re-layouts: 132 us -> 6.86 us
  Pallas kernels: 0 us -> 50 us
  blocking collectives: 24.3 us -> 0 us
  starting transfers between devices: 18.1 us -> 0 us
  between operations: 13.9 us -> 0.66 us
  matrix products: 9.15 us -> 0 us
  other arithmetic: 8.88 us -> 0 us
    psum x1 -> x0, waiting for transfers between devices: 246 us -> none  [body(): grad_second = lax.psum(grad_terms, ('graph', 'feat'))]
    reduce_scatter x1 -> x0, waiting for transfers between devices: 129 us -> none  [body(): lax.psum_scatter(term + jnp.dot(mean_part, w_first[1], preferred_element_...]
    gather x3 -> x0, local copies, waits for them, and re-layouts: 114 us -> none  [the longest x2 113 us: body(): gathered = features[nbr_first].astype(jnp.float32)]
    all_gather x1 -> x0, waiting for transfers between devices: 70.2 us -> none  [body(): piece = lax.all_gather(d_pre, 'feat', axis=0, tiled=True)]
    pallas_call x0 -> x1, Pallas kernels: none -> 50 us  [body(): pl.pallas_call(functools.partial(kernel, n_graph, n_feat), out_shape=(jax...]
    psum x1 -> x0, blocking collectives: 24.3 us -> none  [body(): grad_first = lax.psum(local_grad, 'graph')]
    all_to_all x2 -> x0, starting transfers between devices: 18 us -> none  [the longest x1 10.9 us: body(): lax.all_to_all(halo_grad, 'graph', split_axis=0, concat_axis=0, tiled=True)]
    convert_element_type x2 -> x0, local copies, waits for them, and re-layouts: 13.3 us -> none  [the longest x1 12.7 us: body(): gathered = features[nbr_first].astype(jnp.float32)]
  transfers between devices with their start and end apart: 5 -> 0, of which waited for: 5 -> 0; matrix products, arithmetic and copies ran while one was open for 1% -> 0% of each run, Pallas kernels for 0% -> 0%
where the time goes in v1:
time: 57.9 us; the launch traced here: 57.5 us
  Pallas kernels  50 us (86%)
  local copies, waits for them, and re-layouts  6.86 us (12%)
  between operations  0.66 us (1%)
    pallas_call x1, Pallas kernels, body(): pl.pallas_call(functools.partial(kernel, n_graph, n_feat), out_shape=(jax...  50 us
    unnamed x17, local copies, waits for them, and re-layouts  6.79 us

profile of v1, /device:TPU:1, one launch (start us, length us, event | category | flops | bytes accessed | tf_op | source)
XLA Modules:
  0.0 57.5 jit_solution(1796386519758264736)
XLA Ops:
  0.6 0.0 copy-start.6
  0.6 0.0 copy-start.4
  0.7 0.7 %copy-done.6 = s32[1,8,8]{2,1,0:T(8,128)S(1)} copy-done((s32[1,8,8]{2,1,0:T(8,128)S(1)}, s32[1,8,8]{2,1,0:T(8,128)}, u32[]{:S(2)}) %copy-start.6) | copy-done | bytes 280
  1.3 0.1 reshape.13.send_ref
  1.4 0.0 copy-done.4
  1.4 0.0 copy-start
  1.4 0.9 %copy-done = bf16[2,256,256]{2,1,0:T(8,128)(2,1)S(1)} copy-done((bf16[2,256,256]{2,1,0:T(8,128)(2,1)S(1)}, bf16[2,256,256]{2,1,0:T(8,128)(2,1)}, u32[]{:S(2)}) %copy-start) | copy-done | bytes 262168
  2.4 0.0 copy-start.1
  2.4 0.9 %copy-done.1 = s32[2048,15]{0,1:T(8,128)S(1)} copy-done((s32[2048,15]{0,1:T(8,128)S(1)}, s32[2048,15]{0,1:T(8,128)}, u32[]{:S(2)}) %copy-start.1) | copy-done | bytes 122904
  3.3 0.0 copy-start.2
  3.3 0.8 %copy-done.2 = bf16[4096,8]{0,1:T(8,128)(2,1)S(1)} copy-done((bf16[4096,8]{0,1:T(8,128)(2,1)S(1)}, bf16[4096,8]{0,1:T(8,128)(2,1)}, u32[]{:S(2)}) %copy-start.2) | copy-done | bytes 65560
  4.1 0.0 copy-start.3
  4.1 0.7 %copy-done.3 = bf16[32,256]{1,0:T(8,128)(2,1)S(1)} copy-done((bf16[32,256]{1,0:T(8,128)(2,1)S(1)}, bf16[32,256]{1,0:T(8,128)(2,1)}, u32[]{:S(2)}) %copy-start.3) | copy-done | bytes 16408
  4.8 0.0 copy-start.5
  4.8 0.7 %copy-done.5 = s32[32,10]{0,1:T(8,128)S(1)} copy-done((s32[32,10]{0,1:T(8,128)S(1)}, s32[32,10]{0,1:T(8,128)}, u32[]{:S(2)}) %copy-start.5) | copy-done | bytes 1304
  5.5 50.0 %shard_map.94 = (bf16[32,256]{1,0:T(8,128)(2,1)S(1)}, f32[2,256,256]{2,1,0:T(8,128)S(1)}, f32[2,8,256]{2,1,0:T(8,128)S(1)}) custom-call(bf16[8,4096]{1,0:T(8,128)(2,1)S(1)} %bitcast.5, bf16[16,256]{1,0:T(8,128)(2,1)S(1)} %bitcast.6, bf16[2,256,256]{2,1,0:T(8,128)(2,1)S(1)} %copy-done, bf16[32,256]{1,0:T(8,128)(2,1)S(1)} %copy-done.3, ...), custom_call_target="tpu_custom_call" | custom-call | tf_op jit(solution)/shard_map/pallas_call | solution.py:262
  55.5 0.6 %copy.13 = bf16[32,256]{1,0:T(8,128)(2,1)} copy(bf16[32,256]{1,0:T(8,128)(2,1)S(1)} %get-tuple-element.6) | data formatting | bytes 32768
  56.1 0.8 %copy.14 = f32[2,256,256]{2,1,0:T(8,128)} copy(f32[2,256,256]{2,1,0:T(8,128)S(1)} %get-tuple-element.7) | data formatting | bytes 1048576
  56.9 0.6 %copy.15 = f32[2,8,256]{2,1,0:T(8,128)} copy(f32[2,8,256]{2,1,0:T(8,128)S(1)} %get-tuple-element.8) | data formatting | bytes 32768
Async XLA Ops:
  0.6 0.7 %copy-start.6 = (s32[1,8,8]{2,1,0:T(8,128)S(1)}, s32[1,8,8]{2,1,0:T(8,128)}, u32[]{:S(2)}) copy-start(s32[1,8,8]{2,1,0:T(8,128)} %param.12) | copy-start | bytes 772
  0.6 0.8 %copy-start.4 = (bf16[2,8,256]{2,1,0:T(8,128)(2,1)S(1)}, bf16[2,8,256]{2,1,0:T(8,128)(2,1)}, u32[]{:S(2)}) copy-start(bf16[2,8,256]{2,1,0:T(8,128)(2,1)} %param.8) | copy-start | bytes 24580
  1.4 1.0 %copy-start = (bf16[2,256,256]{2,1,0:T(8,128)(2,1)S(1)}, bf16[2,256,256]{2,1,0:T(8,128)(2,1)}, u32[]{:S(2)}) copy-start(bf16[2,256,256]{2,1,0:T(8,128)(2,1)} %w2_ref.1) | copy-start | bytes 786436
  2.4 0.9 %copy-start.1 = (s32[2048,15]{0,1:T(8,128)S(1)}, s32[2048,15]{0,1:T(8,128)}, u32[]{:S(2)}) copy-start(s32[2048,15]{0,1:T(8,128)} %param.11) | copy-start | bytes 368644
  3.3 0.8 %copy-start.2 = (bf16[4096,8]{0,1:T(8,128)(2,1)S(1)}, bf16[4096,8]{0,1:T(8,128)(2,1)}, u32[]{:S(2)}) copy-start(bf16[4096,8]{0,1:T(8,128)(2,1)} %param.7) | copy-start | bytes 196612
  4.1 0.7 %copy-start.3 = (bf16[32,256]{1,0:T(8,128)(2,1)S(1)}, bf16[32,256]{1,0:T(8,128)(2,1)}, u32[]{:S(2)}) copy-start(bf16[32,256]{1,0:T(8,128)(2,1)} %cot_ref.1) | copy-start | bytes 49156
  4.8 0.7 %copy-start.5 = (s32[32,10]{0,1:T(8,128)S(1)}, s32[32,10]{0,1:T(8,128)}, u32[]{:S(2)}) copy-start(s32[32,10]{0,1:T(8,128)} %param.13) | copy-start | bytes 3844

commit v2 on v1

v2 whole, which is shorter than its diff:
```python
import functools

import jax
import jax.numpy as jnp
from jax import lax
from jax.experimental import pallas as pl
from jax.experimental.pallas import tpu as pltpu
from jax.sharding import PartitionSpec as P

HID = 256
FAN1 = 15
FAN2 = 10
OWN = 32
HALO = 8
SRC = 4096
N_X = 4
LO = 256
GROUPS = SRC // LO
BF16 = jnp.bfloat16
F32 = jnp.float32
MESH = pl.DeviceIdType.MESH


def select_tree(values, masks):
    for mask in masks:
        values = [
            jnp.where(mask, values[2 * i + 1], values[2 * i]) for i in range(len(values) // 2)
        ]
    return values[0]


def dot(a, b):
    return jnp.dot(a, b, preferred_element_type=F32)


def dot_lhs_t(a, b):
    return lax.dot_general(a, b, (((0,), (0,)), ((), ())), preferred_element_type=F32)


def dot_rhs_t(a, b):
    return lax.dot_general(a, b, (((1,), (1,)), ((), ())), preferred_element_type=F32)


def outward(n, i):
    return n // 2 + (1 - 2 * (i % 2)) * ((i + 1) // 2)


def split(a):
    high = a.astype(BF16)
    return high, (a - high.astype(F32)).astype(BF16)


def kernel(
    n_graph, n_feat,
    feat_hbm, w1_hbm, w2_hbm, cot_hbm, near1_hbm, send_hbm, near2_hbm,
    out_ref, g2_ref, g1_ref,
    feat_ref, near1_ref, w2_ref, cot_ref, send_ref, near2_ref,
    table, x_own, x_all, w_all, pre_part, pre_in, d_all, hid_own, hid_in,
    v_out, v_in, e_out, e_in, hh_out, hh_in,
    gs_out, gs_in, gz, gz_in, gfin, gsib, dw_out, dw_in, dz, dz_in,
    send_sem, recv_sem, load_sem,
):
    n_chip = n_feat // 2
    n_row = n_feat // 4
    n_y = n_chip // N_X
    n_m = n_y // 2
    targets = n_feat * OWN
    tile = targets // 2
    shard = HID // n_chip
    g = lax.axis_index("graph")
    f = lax.axis_index("feat")
    row, part = f // 4, f % 4
    chip, core = f // 2, f % 2
    sibling = f + 1 - 2 * core

    def chip_at(i):
        x = (chip // n_y + outward(N_X, i % N_X)) % N_X
        y = (chip % n_y + outward(n_y, i // N_X)) % n_y
        return x * n_y + y

    def row_at(i, sign):
        x = (row // n_m + sign * outward(N_X, i % N_X) + N_X) % N_X
        m = (row % n_m + sign * outward(n_m, i // N_X) + n_m) % n_m
        return x * n_m + m

    def graph_at(i):
        return (g + outward(n_graph, i)) % n_graph

    def remote(index, src, dst, graph, feat):
        return pltpu.make_async_remote_copy(
            src_ref=src, dst_ref=dst, send_sem=send_sem.at[index], recv_sem=recv_sem.at[index],
            device_id=(graph, feat), device_id_type=MESH,
        )

    def wait_in(index, ref):
        remote(index, ref, ref, g, sibling).wait_recv()

    def wait_out(index, ref):
        remote(index, ref, ref, g, sibling).wait_send()

    def loop(high, step):
        def body(i, carry):
            step(i)
            return carry

        lax.fori_loop(0, high, body, 0)

    loads = [
        pltpu.make_async_copy(src, dst, load_sem.at[i])
        for i, (src, dst) in enumerate((
            (feat_hbm, feat_ref), (near1_hbm, near1_ref), (w1_hbm, w_all.at[n_row - 1]), (cot_hbm, cot_ref),
            (near2_hbm, near2_ref), (send_hbm, send_ref), (w2_hbm, w2_ref),
        ))
    ]
    for load in loads:
        load.start()

    barrier = pltpu.get_barrier_semaphore()

    def greet(graph, feat):
        pl.semaphore_signal(barrier, inc=1, device_id=(graph, feat), device_id_type=MESH)

    loop(n_chip - 1, lambda i: greet(g, 2 * chip_at(i) + core))
    loop(n_graph - 1, lambda i: greet(graph_at(i), f))
    greet(g, 4 * row + 3 - part)
    greet(g, sibling)

    loads[0].wait()
    loads[1].wait()
    for s in range(GROUPS):
        table[s * 8 : (s + 1) * 8, :] = feat_ref[:, s * LO : (s + 1) * LO].astype(F32)
    lows = lax.broadcasted_iota(jnp.int32, (LO, tile), 0).astype(F32).astype(BF16)

    def gather(t):
        columns = pl.ds(pl.multiple_of(t * tile, tile), tile)
        near = near1_ref[:, columns]
        groups = table[...].astype(BF16)
        total = jnp.zeros((8, tile), F32)
        for k in range(FAN1):
            index = near[k : k + 1]
            low = jnp.broadcast_to((index % LO).astype(F32), (16, tile)).astype(BF16)
            low = jnp.concatenate([low] * (LO // 16), axis=0)
            picked = dot(groups, jnp.where(lows == low, jnp.ones((), BF16), jnp.zeros((), BF16)))
            high = jnp.broadcast_to(index // LO, (8, tile))
            masks = [(high // (1 << bit)) % 2 != 0 for bit in range(4)]
            total = total + select_tree([picked[s * 8 : (s + 1) * 8] for s in range(GROUPS)], masks)
        both = jnp.concatenate([feat_ref[:, columns].astype(F32), total / FAN1], axis=0).astype(BF16)
        for i in range(tile // 128):
            x_own[t * (tile // 128) + i] = both[:, i * 128 : (i + 1) * 128]

    def step(t):
        gather(t)

        @pl.when(t == 0)
        def _():
            pl.semaphore_wait(barrier, n_chip - 1 + n_graph - 1 + 2)
            loads[2].wait()
            own = w_all.at[n_row - 1]
            loop(n_row - 1, lambda i: remote(0, own, w_all.at[i], g, 4 * row_at(i, 1) + part).start())

        def send_x(i):
            block = row_at(i, 1)

            @pl.when(block // (n_row // 2) == t)
            def _():
                remote(1, x_own.at[block], x_all.at[i], g, 4 * block + part).start()

        loop(n_row - 1, send_x)

    loop(2, step)
    x_all[n_row - 1] = x_own[row]

    for load in loads[3:]:
        load.wait()
    width = OWN + n_graph * HALO
    near2 = near2_ref[...]
    slots = lax.broadcasted_iota(jnp.int32, (width, OWN), 0)
    counts_t = jnp.zeros((width, OWN), F32)
    for k in range(FAN2):
        counts_t = counts_t + jnp.where(slots == near2[k : k + 1], 1.0, 0.0)
    counts_t = counts_t.astype(BF16)
    cot = cot_ref[...]
    e_all = dot(counts_t, cot)
    e_out[...] = e_all[OWN:].reshape(n_graph, HALO, HID)
    loop(n_graph - 1, lambda i: remote(2, e_out.at[graph_at(i)], e_in.at[g], graph_at(i), f).start())
    rows = lax.broadcasted_iota(jnp.int32, (OWN, n_graph * HALO), 0)
    sent = send_ref[...]
    sent = jnp.concatenate([sent[p : p + 1] for p in range(n_graph)], axis=1)
    pick_t = jnp.where(rows == sent, 1.0, 0.0).astype(BF16)

    wait_in(0, w_all.at[pl.ds(0, n_row - 1)])
    wait_in(1, x_all.at[pl.ds(0, n_row - 1)])
    x = x_all[...].reshape(n_row * 16, 128)
    pre_part[...] = dot_lhs_t(x, w_all[...].reshape(n_row * 16, HID)).reshape(4, OWN, HID)
    for d in (2, 1, 3):
        remote(4, pre_part.at[(part + d) % 4], pre_in.at[d], g, 4 * row + (part + d) % 4).start()

    e_in[g] = jnp.zeros((HALO, HID), F32)
    wait_in(2, e_in.at[pl.ds(0, n_graph - 1)])
    back = e_in[...].reshape(n_graph * HALO, HID)
    back_high, back_low = split(back)
    e_total = (e_all[:OWN] + (dot(pick_t, back_high) + dot(pick_t, back_low))) / FAN2
    e_high, e_low = split(e_total)
    first = jnp.broadcast_to(core, (OWN, HID)) == 0
    cot32, e32 = cot.astype(F32), e_high.astype(F32)
    v_own = jnp.where(first, cot32, e32).astype(BF16)
    v_out[...] = jnp.where(first, e32, cot32).astype(BF16)
    remote(3, v_out, v_in, g, sibling).start()
    d_hidden = dot_rhs_t(cot, w2_ref[0]) + (dot_rhs_t(e_high, w2_ref[1]) + dot_rhs_t(e_low, w2_ref[1]))

    wait_in(4, pre_in.at[pl.ds(1, 3)])
    pre = (pre_part[part] + pre_in[1]) + (pre_in[2] + pre_in[3])
    sig = 1.0 / (1.0 + jnp.exp(-pre))
    hidden = (pre * sig).astype(BF16)
    hid_own[...] = hidden
    remote(5, hid_own, hid_in, g, sibling).start()
    d_all[part] = (d_hidden * (sig * (1.0 + pre * (1.0 - sig)))).astype(BF16)
    for d in (2, 1, 3):
        remote(6, d_all.at[part], d_all.at[part], g, 4 * row + (part + d) % 4).start()

    wait_in(3, v_in)
    v_pair = jnp.concatenate([v_own, v_in[...]], axis=0)
    wait_in(5, hid_in)
    grad = dot_lhs_t(jnp.concatenate([hidden, hid_in[...]], axis=0), v_pair).reshape(n_chip, shard, HID)
    gs_out[...] = jnp.concatenate([grad[:, :, :128], grad[:, :, 128:]], axis=1).astype(BF16)

    def send_grad(i):
        peer = chip_at(i)
        remote(8, gs_out.at[peer], gs_in.at[i], g, 2 * peer + core).start()

    loop(n_chip - 1, send_grad)
    gs_in[n_chip - 1] = gs_out[chip]

    hh_out[...] = dot_lhs_t(pick_t, hidden).reshape(n_graph, HALO, HID)
    loop(n_graph - 1, lambda i: remote(7, hh_out.at[graph_at(i)], hh_in.at[g], graph_at(i), f).start())

    wait_in(6, d_all.at[pl.ds(0, 3)])
    dw_out[...] = dot(x, d_all[...].reshape(4 * OWN, HID)).reshape(n_row, 16, HID).astype(BF16)
    loop(n_row - 1, lambda i: remote(9, dw_out.at[i], dw_in.at[i], g, 4 * row_at(i, -1) + part).start())
    dw_in[n_row - 1] = dw_out[n_row - 1]

    wait_in(8, gs_in.at[pl.ds(0, n_chip - 1)])
    gz[...] = jnp.sum(gs_in[...].astype(F32), axis=0)
    loop(n_graph - 1, lambda i: remote(10, gz, gz_in.at[g], graph_at(i), f).start())
    gz_in[g] = gz[...]

    hh_in[g] = jnp.zeros((HALO, HID), F32)
    wait_in(7, hh_in.at[pl.ds(0, n_graph - 1)])
    ext = jnp.concatenate([hidden.astype(F32), hh_in[...].reshape(n_graph * HALO, HID)], axis=0).astype(BF16)
    mean2 = (dot_lhs_t(counts_t, ext) / FAN2).astype(BF16)
    out_ref[...] = (dot(hidden, w2_ref[0]) + dot(mean2, w2_ref[1])).astype(BF16)

    wait_in(10, gz_in.at[pl.ds(0, n_graph - 1)])
    gfin[chip] = jnp.sum(gz_in[...], axis=0).astype(BF16)
    loop(n_chip - 1, lambda i: remote(11, gfin.at[chip], gfin.at[chip], g, 2 * chip_at(i) + core).start())

    wait_in(9, dw_in.at[pl.ds(0, n_row - 1)])
    dz[...] = jnp.sum(dw_in[...].astype(F32), axis=0)
    dz_in[g] = dz[...]
    loop(n_graph - 1, lambda i: remote(12, dz, dz_in.at[g], graph_at(i), f).start())
    wait_in(12, dz_in.at[pl.ds(0, n_graph - 1)])
    g1_ref[...] = jnp.sum(dz_in[...], axis=0).reshape(2, 8, HID)

    def unpack(ref, which):
        both = ref[...].astype(F32)
        g2_ref[which, :, 0:128] = both[:, :shard].reshape(HID, 128)
        g2_ref[which, :, 128:256] = both[:, shard:].reshape(HID, 128)

    wait_in(11, gfin.at[pl.ds(0, n_chip - 1)])
    remote(13, gfin, gsib, g, sibling).start()
    unpack(gfin, core)
    wait_in(13, gsib)
    unpack(gsib, 1 - core)

    wait_out(0, w_all.at[pl.ds(0, n_row - 1)])
    wait_out(1, x_all.at[pl.ds(0, n_row - 1)])
    wait_out(2, e_in.at[pl.ds(0, n_graph - 1)])
    wait_out(3, v_in)
    wait_out(4, pre_in.at[pl.ds(1, 3)])
    wait_out(5, hid_in)
    wait_out(6, d_all.at[pl.ds(0, 3)])
    wait_out(7, hh_in.at[pl.ds(0, n_graph - 1)])
    wait_out(8, gs_in.at[pl.ds(0, n_chip - 1)])
    wait_out(9, dw_in.at[pl.ds(0, n_row - 1)])
    wait_out(10, gz_in.at[pl.ds(0, n_graph - 1)])
    wait_out(11, gfin.at[pl.ds(0, n_chip - 1)])
    wait_out(12, dz_in.at[pl.ds(0, n_graph - 1)])
    wait_out(13, gsib)


def store_kernel(a_ref, b_ref, c_ref, a_out, b_out, c_out, sem):
    copies = [
        pltpu.make_async_copy(src, dst, sem.at[i])
        for i, (src, dst) in enumerate(((b_ref, b_out), (a_ref, a_out), (c_ref, c_out)))
    ]
    for copy in copies:
        copy.start()
    for copy in copies:
        copy.wait()


def solution(mesh):
    n_graph, n_feat = mesh.shape["graph"], mesh.shape["feat"]
    n_chip, n_row = n_feat // 2, n_feat // 4
    pack = 2 * HID // n_chip

    def body(features, w_first, w_second, cotangent, nbr_first, send_rows, nbr_second):
        vmem = pl.BlockSpec(memory_space=pltpu.VMEM)
        hbm = pl.BlockSpec(memory_space=pltpu.HBM)
        shapes = (
            jax.ShapeDtypeStruct((OWN, HID), BF16),
            jax.ShapeDtypeStruct((2, HID, HID), F32),
            jax.ShapeDtypeStruct((2, 8, HID), F32),
        )
        results = pl.pallas_call(
            functools.partial(kernel, n_graph, n_feat),
            out_shape=shapes,
            in_specs=[hbm] * 7,
            out_specs=(vmem,) * 3,
            scratch_shapes=[
                pltpu.VMEM((8, SRC), BF16),
                pltpu.VMEM((FAN1, n_feat * OWN), jnp.int32),
                pltpu.VMEM((2, HID, HID), BF16),
                pltpu.VMEM((OWN, HID), BF16),
                pltpu.VMEM((n_graph, HALO), jnp.int32),
                pltpu.VMEM((FAN2, OWN), jnp.int32),
                pltpu.VMEM((GROUPS * 8, LO), F32),
                pltpu.VMEM((n_row, 16, 128), BF16),
                pltpu.VMEM((n_row, 16, 128), BF16),
                pltpu.VMEM((n_row, 16, HID), BF16),
                pltpu.VMEM((4, OWN, HID), F32),
                pltpu.VMEM((4, OWN, HID), F32),
                pltpu.VMEM((4, OWN, HID), BF16),
                pltpu.VMEM((OWN, HID), BF16),
                pltpu.VMEM((OWN, HID), BF16),
                pltpu.VMEM((OWN, HID), BF16),
                pltpu.VMEM((OWN, HID), BF16),
                pltpu.VMEM((n_graph, HALO, HID), F32),
                pltpu.VMEM((n_graph, HALO, HID), F32),
                pltpu.VMEM((n_graph, HALO, HID), F32),
                pltpu.VMEM((n_graph, HALO, HID), F32),
                pltpu.VMEM((n_chip, pack, 128), BF16),
                pltpu.VMEM((n_chip, pack, 128), BF16),
                pltpu.VMEM((pack, 128), F32),
                pltpu.VMEM((n_graph, pack, 128), F32),
                pltpu.VMEM((n_chip, pack, 128), BF16),
                pltpu.VMEM((n_chip, pack, 128), BF16),
                pltpu.VMEM((n_row, 16, HID), BF16),
                pltpu.VMEM((n_row, 16, HID), BF16),
                pltpu.VMEM((16, HID), F32),
                pltpu.VMEM((n_graph, 16, HID), F32),
                pltpu.SemaphoreType.DMA((14,)),
                pltpu.SemaphoreType.DMA((14,)),
                pltpu.SemaphoreType.DMA((7,)),
            ],
            compiler_params=pltpu.CompilerParams(
                collective_id=0, has_side_effects=True, vmem_limit_bytes=40 * 1024 * 1024
            ),
        )(
            *(
                pltpu.with_memory_space_constraint(a, pltpu.HBM)
                for a in (
                    features.T,
                    w_first.reshape(16, HID),
                    w_second,
                    cotangent,
                    nbr_first.T,
                    send_rows.reshape(n_graph, HALO),
                    nbr_second.T,
                )
            )
        )
        return pl.pallas_call(
            store_kernel,
            out_shape=shapes,
            in_specs=[vmem] * 3,
            out_specs=(hbm,) * 3,
            scratch_shapes=[pltpu.SemaphoreType.DMA((3,))],
        )(*results)

    in_specs = (
        P("graph", "feat"),
        P(None, "feat", None),
        P(),
        P(("graph", "feat"), None),
        P("graph", None),
        P(("graph", "feat"), None, None),
        P(("graph", "feat"), None),
    )
    out_specs = (P(("graph", "feat"), None), P(), P(None, "feat", None))
    return jax.shard_map(body, mesh=mesh, in_specs=in_specs, out_specs=out_specs, check_vma=False)
```

time: 57.9 us -> 54.3 us (0.938)
  local copies, waits for them, and re-layouts: 6.86 us -> 1.97 us
  Pallas kernels: 50 us -> 51.5 us
    unnamed x17 -> x6, local copies, waits for them, and re-layouts: 6.79 us -> 1.97 us
    pallas_call x1 -> x2, Pallas kernels: 50 us -> 51.5 us  [the longest x1 49.7 us: body(): pl.pallas_call(functools.partial(kernel, n_graph, n_feat), out_shape=shap...]
where the time goes in v2:
time: 54.3 us; the launch traced here: 54.2 us
  Pallas kernels  51.5 us (95%)
  local copies, waits for them, and re-layouts  1.97 us (4%)
  between operations  0.65 us (1%)
    pallas_call x1, Pallas kernels, body(): pl.pallas_call(functools.partial(kernel, n_graph, n_feat), out_shape=shap...  49.7 us
    unnamed x6, local copies, waits for them, and re-layouts  1.97 us
    pallas_call x1, Pallas kernels, body(): pl.pallas_call(store_kernel, out_shape=shapes, in_specs=[vmem] * 3, out_s...  1.86 us

profile of v2, /device:TPU:1, one launch (start us, length us, event | category | flops | bytes accessed | tf_op | source)
XLA Modules:
  0.0 54.2 jit_solution(3547785906306303128)
XLA Ops:
  0.6 49.7 %shard_map.94 = (bf16[32,256]{1,0:T(8,128)(2,1)S(1)}, f32[2,256,256]{2,1,0:T(8,128)S(1)}, f32[2,8,256]{2,1,0:T(8,128)S(1)}) custom-call(bf16[8,4096]{1,0:T(8,128)(2,1)} %bitcast.6, bf16[16,256]{1,0:T(8,128)(2,1)} %bitcast.7, bf16[2,256,256]{2,1,0:T(8,128)(2,1)} %w2_hbm.1, bf16[32,256]{1,0:T(8,128)(2,1)} %cot_hbm.1, s32[15,2048]{1,0:T(8,128)} %bitcast.5, ...), custom_call_target="tpu_custom_call" | custom-call | tf_op jit(solution)/shard_map/pallas_call | solution.py:315
  50.3 0.0 copy-start
  50.3 0.8 %copy-done = f32[2,256,256]{2,1,0:T(8,128)} copy-done((f32[2,256,256]{2,1,0:T(8,128)}, f32[2,256,256]{2,1,0:T(8,128)S(1)}, u32[]{:S(2)}) %copy-start) | copy-done | bytes 524312
  51.1 0.0 copy-start.1
  51.1 0.6 %copy-done.1 = bf16[32,256]{1,0:T(8,128)(2,1)} copy-done((bf16[32,256]{1,0:T(8,128)(2,1)}, bf16[32,256]{1,0:T(8,128)(2,1)S(1)}, u32[]{:S(2)}) %copy-start.1) | copy-done | bytes 16408
  51.7 0.0 copy-start.2
  51.7 0.6 %copy-done.2 = f32[2,8,256]{2,1,0:T(8,128)} copy-done((f32[2,8,256]{2,1,0:T(8,128)}, f32[2,8,256]{2,1,0:T(8,128)S(1)}, u32[]{:S(2)}) %copy-start.2) | copy-done | bytes 16408
  52.3 1.9 %shard_map.95 = (bf16[32,256]{1,0:T(8,128)(2,1)}, f32[2,256,256]{2,1,0:T(8,128)}, f32[2,8,256]{2,1,0:T(8,128)}) custom-call(bf16[32,256]{1,0:T(8,128)(2,1)} %copy-done.1, f32[2,256,256]{2,1,0:T(8,128)} %copy-done, f32[2,8,256]{2,1,0:T(8,128)} %copy-done.2), custom_call_target="tpu_custom_call" | custom-call | tf_op jit(solution)/shard_map/pallas_call | solution.py:373
Async XLA Ops:
  50.3 0.8 %copy-start = (f32[2,256,256]{2,1,0:T(8,128)}, f32[2,256,256]{2,1,0:T(8,128)S(1)}, u32[]{:S(2)}) copy-start(f32[2,256,256]{2,1,0:T(8,128)S(1)} %get-tuple-element.7.b_ref) | copy-start | bytes 1572868
  51.1 0.6 %copy-start.1 = (bf16[32,256]{1,0:T(8,128)(2,1)}, bf16[32,256]{1,0:T(8,128)(2,1)S(1)}, u32[]{:S(2)}) copy-start(bf16[32,256]{1,0:T(8,128)(2,1)S(1)} %get-tuple-element.6.a_ref) | copy-start | bytes 49156
  51.7 0.6 %copy-start.2 = (f32[2,8,256]{2,1,0:T(8,128)}, f32[2,8,256]{2,1,0:T(8,128)S(1)}, u32[]{:S(2)}) copy-start(f32[2,8,256]{2,1,0:T(8,128)S(1)} %get-tuple-element.8.c_ref) | copy-start | bytes 49156

commit v3 on v2

--- a/solution.py
+++ b/solution.py
@@ -72,19 +72,30 @@
     row, part = f // 4, f % 4
     chip, core = f // 2, f % 2
     sibling = f + 1 - 2 * core
-
-    def chip_at(i):
-        x = (chip // n_y + outward(N_X, i % N_X)) % N_X
-        y = (chip % n_y + outward(n_y, i // N_X)) % n_y
-        return x * n_y + y
-
-    def row_at(i, sign):
-        x = (row // n_m + sign * outward(N_X, i % N_X) + N_X) % N_X
-        m = (row % n_m + sign * outward(n_m, i // N_X) + n_m) % n_m
-        return x * n_m + m
-
-    def graph_at(i):
-        return (g + outward(n_graph, i)) % n_graph
+    x, y = chip // n_y, chip % n_y
+    sheet = x * n_y + (1 - core) * y + core * g
+
+    depth = (1 - core) * y + core * g
+    around = (1 - core) * g + core * y
+    turn_x = [(x + outward(N_X, i)) % N_X for i in range(N_X)]
+    turn_d = [(depth + outward(n_y, i)) % n_y for i in range(n_y)]
+    turn_a = [(around + outward(n_y, i)) % n_y for i in range(n_y)]
+    turn_m = [(row % n_m + outward(n_m, i)) % n_m for i in range(n_m)]
+    back_x = [(x - outward(N_X, i) + N_X) % N_X for i in range(N_X)]
+    back_m = [(row % n_m - outward(n_m, i) + n_m) % n_m for i in range(n_m)]
+    graphs = [(g + outward(n_graph, i)) % n_graph for i in range(n_graph - 1)]
+    sheet_x = [2 * n_y * to + core for to in turn_x]
+    sheet_f = [2 * ((1 - core) * to + core * y) for to in turn_d]
+    sheet_g = [(1 - core) * g + core * to for to in turn_d]
+    sheet_peers = [
+        (turn_x[i % N_X] * n_y + turn_d[i // N_X], sheet_g[i // N_X], sheet_x[i % N_X] + sheet_f[i // N_X])
+        for i in range(n_chip - 1)
+    ]
+    ring_peers = [
+        ((1 - core) * to + core * g, 2 * (x * n_y + (1 - core) * y + core * to) + core) for to in turn_a[:-1]
+    ]
+    row_peers = [turn_x[i % N_X] * n_m + turn_m[i // N_X] for i in range(n_row - 1)]
+    row_sources = [back_x[i % N_X] * n_m + back_m[i // N_X] for i in range(n_row - 1)]
 
     def remote(index, src, dst, graph, feat):
         return pltpu.make_async_remote_copy(
@@ -97,13 +108,6 @@
 
     def wait_out(index, ref):
         remote(index, ref, ref, g, sibling).wait_send()
-
-    def loop(high, step):
-        def body(i, carry):
-            step(i)
-            return carry
-
-        lax.fori_loop(0, high, body, 0)
 
     loads = [
         pltpu.make_async_copy(src, dst, load_sem.at[i])
@@ -120,8 +124,17 @@
     def greet(graph, feat):
         pl.semaphore_signal(barrier, inc=1, device_id=(graph, feat), device_id_type=MESH)
 
-    loop(n_chip - 1, lambda i: greet(g, 2 * chip_at(i) + core))
-    loop(n_graph - 1, lambda i: greet(graph_at(i), f))
+    for _, graph, feat in sheet_peers:
+        greet(graph, feat)
+    for graph, feat in ring_peers:
+        greet(graph, feat)
+
+    @pl.when(core == 1)
+    def _():
+        for i in range(n_row - 1):
+            if i % N_X != N_X - 1:
+                greet(g, 4 * row_peers[i] + part)
+
     greet(g, 4 * row + 3 - part)
     greet(g, sibling)
 
@@ -148,26 +161,26 @@
         for i in range(tile // 128):
             x_own[t * (tile // 128) + i] = both[:, i * 128 : (i + 1) * 128]
 
-    def step(t):
+    def step(t, carry):
         gather(t)
 
         @pl.when(t == 0)
         def _():
-            pl.semaphore_wait(barrier, n_chip - 1 + n_graph - 1 + 2)
+            pl.semaphore_wait(barrier, n_chip - 1 + n_graph - 1 + 2 + core * (n_row - n_row // N_X))
             loads[2].wait()
             own = w_all.at[n_row - 1]
-            loop(n_row - 1, lambda i: remote(0, own, w_all.at[i], g, 4 * row_at(i, 1) + part).start())
-
-        def send_x(i):
-            block = row_at(i, 1)
+            for i, peer in enumerate(row_peers):
+                remote(0, own, w_all.at[i], g, 4 * peer + part).start()
+
+        for i, block in enumerate(row_peers):
 
             @pl.when(block // (n_row // 2) == t)
-            def _():
+            def _(i=i, block=block):
                 remote(1, x_own.at[block], x_all.at[i], g, 4 * block + part).start()
 
-        loop(n_row - 1, send_x)
-
-    loop(2, step)
+        return carry
+
+    lax.fori_loop(0, 2, step, 0)
     x_all[n_row - 1] = x_own[row]
 
     for load in loads[3:]:
@@ -182,7 +195,8 @@
     cot = cot_ref[...]
     e_all = dot(counts_t, cot)
     e_out[...] = e_all[OWN:].reshape(n_graph, HALO, HID)
-    loop(n_graph - 1, lambda i: remote(2, e_out.at[graph_at(i)], e_in.at[g], graph_at(i), f).start())
+    for peer in graphs:
+        remote(2, e_out.at[peer], e_in.at[g], peer, f).start()
     rows = lax.broadcasted_iota(jnp.int32, (OWN, n_graph * HALO), 0)
     sent = send_ref[...]
     sent = jnp.concatenate([sent[p : p + 1] for p in range(n_graph)], axis=1)
@@ -190,8 +204,8 @@
 
     wait_in(0, w_all.at[pl.ds(0, n_row - 1)])
     wait_in(1, x_all.at[pl.ds(0, n_row - 1)])
-    x = x_all[...].reshape(n_row * 16, 128)
-    pre_part[...] = dot_lhs_t(x, w_all[...].reshape(n_row * 16, HID)).reshape(4, OWN, HID)
+    inputs = x_all[...].reshape(n_row * 16, 128)
+    pre_part[...] = dot_lhs_t(inputs, w_all[...].reshape(n_row * 16, HID)).reshape(4, OWN, HID)
     for d in (2, 1, 3):
         remote(4, pre_part.at[(part + d) % 4], pre_in.at[d], g, 4 * row + (part + d) % 4).start()
 
@@ -224,25 +238,25 @@
     grad = dot_lhs_t(jnp.concatenate([hidden, hid_in[...]], axis=0), v_pair).reshape(n_chip, shard, HID)
     gs_out[...] = jnp.concatenate([grad[:, :, :128], grad[:, :, 128:]], axis=1).astype(BF16)
 
-    def send_grad(i):
-        peer = chip_at(i)
-        remote(8, gs_out.at[peer], gs_in.at[i], g, 2 * peer + core).start()
-
-    loop(n_chip - 1, send_grad)
-    gs_in[n_chip - 1] = gs_out[chip]
+    for i, (peer, graph, feat) in enumerate(sheet_peers):
+        remote(8, gs_out.at[peer], gs_in.at[i], graph, feat).start()
+    gs_in[n_chip - 1] = gs_out[sheet]
 
     hh_out[...] = dot_lhs_t(pick_t, hidden).reshape(n_graph, HALO, HID)
-    loop(n_graph - 1, lambda i: remote(7, hh_out.at[graph_at(i)], hh_in.at[g], graph_at(i), f).start())
+    for peer in graphs:
+        remote(7, hh_out.at[peer], hh_in.at[g], peer, f).start()
 
     wait_in(6, d_all.at[pl.ds(0, 3)])
-    dw_out[...] = dot(x, d_all[...].reshape(4 * OWN, HID)).reshape(n_row, 16, HID).astype(BF16)
-    loop(n_row - 1, lambda i: remote(9, dw_out.at[i], dw_in.at[i], g, 4 * row_at(i, -1) + part).start())
+    dw_out[...] = dot(inputs, d_all[...].reshape(4 * OWN, HID)).reshape(n_row, 16, HID).astype(BF16)
+    for i, peer in enumerate(row_sources):
+        remote(9, dw_out.at[i], dw_in.at[i], g, 4 * peer + part).start()
     dw_in[n_row - 1] = dw_out[n_row - 1]
 
     wait_in(8, gs_in.at[pl.ds(0, n_chip - 1)])
     gz[...] = jnp.sum(gs_in[...].astype(F32), axis=0)
-    loop(n_graph - 1, lambda i: remote(10, gz, gz_in.at[g], graph_at(i), f).start())
-    gz_in[g] = gz[...]
+    for graph, feat in ring_peers:
+        remote(10, gz, gz_in.at[around], graph, feat).start()
+    gz_in[around] = gz[...]
 
     hh_in[g] = jnp.zeros((HALO, HID), F32)
     wait_in(7, hh_in.at[pl.ds(0, n_graph - 1)])
@@ -251,13 +265,15 @@
     out_ref[...] = (dot(hidden, w2_ref[0]) + dot(mean2, w2_ref[1])).astype(BF16)
 
     wait_in(10, gz_in.at[pl.ds(0, n_graph - 1)])
-    gfin[chip] = jnp.sum(gz_in[...], axis=0).astype(BF16)
-    loop(n_chip - 1, lambda i: remote(11, gfin.at[chip], gfin.at[chip], g, 2 * chip_at(i) + core).start())
+    gfin[sheet] = jnp.sum(gz_in[...], axis=0).astype(BF16)
+    for _, graph, feat in sheet_peers:
+        remote(11, gfin.at[sheet], gfin.at[sheet], graph, feat).start()
 
     wait_in(9, dw_in.at[pl.ds(0, n_row - 1)])
     dz[...] = jnp.sum(dw_in[...].astype(F32), axis=0)
     dz_in[g] = dz[...]
-    loop(n_graph - 1, lambda i: remote(12, dz, dz_in.at[g], graph_at(i), f).start())
+    for peer in graphs:
+        remote(12, dz, dz_in.at[g], peer, f).start()
     wait_in(12, dz_in.at[pl.ds(0, n_graph - 1)])
     g1_ref[...] = jnp.sum(dz_in[...], axis=0).reshape(2, 8, HID)
 
@@ -314,7 +330,7 @@
         )
         results = pl.pallas_call(
             functools.partial(kernel, n_graph, n_feat),
-            out_shape=shapes,
+            out_shape=tuple(pltpu.VMEM(a.shape, a.dtype) for a in shapes),
             in_specs=[hbm] * 7,
             out_specs=(vmem,) * 3,
             scratch_shapes=[
@@ -376,7 +392,7 @@
             in_specs=[vmem] * 3,
             out_specs=(hbm,) * 3,
             scratch_shapes=[pltpu.SemaphoreType.DMA((3,))],
-        )(*results)
+        )(*(pltpu.with_memory_space_constraint(a, pltpu.VMEM) for a in results))
 
     in_specs = (
         P("graph", "feat"),

time: 54.3 us -> 49.3 us (0.908)
  Pallas kernels: 51.5 us -> 48.6 us
  local copies, waits for them, and re-layouts: 1.97 us -> 0 us
    unnamed x6 -> x0, local copies, waits for them, and re-layouts: 1.97 us -> none
    pallas_call x1, Pallas kernels: 49.7 us -> 47.7 us  [body(): pl.pallas_call(functools.partial(kernel, n_graph, n_feat), out_shape=tupl...]
    pallas_call x1, Pallas kernels: 1.86 us -> 0.83 us  [body(): pl.pallas_call(store_kernel, out_shape=shapes, in_specs=[vmem] * 3, out_s...]
where the time goes in v3:
time: 49.3 us; the launch traced here: 49.2 us
  Pallas kernels  48.6 us (99%)
  between operations  0.64 us (1%)
    pallas_call x1, Pallas kernels, body(): pl.pallas_call(functools.partial(kernel, n_graph, n_feat), out_shape=tupl...  47.7 us

profile of v3, /device:TPU:1, one launch (start us, length us, event | category | flops | bytes accessed | tf_op | source)
XLA Modules:
  0.0 49.2 jit_solution(8878850498365089903)
XLA Ops:
  0.6 47.7 %shard_map.94 = (bf16[32,256]{1,0:T(8,128)(2,1)S(1)}, f32[2,256,256]{2,1,0:T(8,128)S(1)}, f32[2,8,256]{2,1,0:T(8,128)S(1)}) custom-call(bf16[8,4096]{1,0:T(8,128)(2,1)} %bitcast.6, bf16[16,256]{1,0:T(8,128)(2,1)} %bitcast.7, bf16[2,256,256]{2,1,0:T(8,128)(2,1)} %w2_hbm.1, bf16[32,256]{1,0:T(8,128)(2,1)} %cot_hbm.1, s32[15,2048]{1,0:T(8,128)} %bitcast.5, ...), custom_call_target="tpu_custom_call" | custom-call | tf_op jit(solution)/shard_map/pallas_call | solution.py:331
  48.4 0.8 %shard_map.95 = (bf16[32,256]{1,0:T(8,128)(2,1)}, f32[2,256,256]{2,1,0:T(8,128)}, f32[2,8,256]{2,1,0:T(8,128)}) custom-call(bf16[32,256]{1,0:T(8,128)(2,1)S(1)} %get-tuple-element.6.a_ref, f32[2,256,256]{2,1,0:T(8,128)S(1)} %get-tuple-element.7.b_ref, f32[2,8,256]{2,1,0:T(8,128)S(1)} %get-tuple-element.8.c_ref), custom_call_target="tpu_custom_call" | custom-call | tf_op jit(solution)/shard_map/pallas_call | solution.py:389

commit v4 on v3

v4 whole, which is shorter than its diff:
```python
import functools

import jax
import jax.numpy as jnp
from jax import lax
from jax.experimental import pallas as pl
from jax.experimental.pallas import tpu as pltpu
from jax.sharding import PartitionSpec as P

HID = 256
FAN1 = 15
FAN2 = 10
OWN = 32
HALO = 8
SRC = 4096
N_X = 4
LO = 256
GROUPS = SRC // LO
BF16 = jnp.bfloat16
F32 = jnp.float32
MESH = pl.DeviceIdType.MESH


def select_tree(values, masks):
    for mask in masks:
        values = [
            jnp.where(mask, values[2 * i + 1], values[2 * i]) for i in range(len(values) // 2)
        ]
    return values[0]


def dot(a, b):
    return jnp.dot(a, b, preferred_element_type=F32)


def dot_lhs_t(a, b):
    return lax.dot_general(a, b, (((0,), (0,)), ((), ())), preferred_element_type=F32)


def dot_rhs_t(a, b):
    return lax.dot_general(a, b, (((1,), (1,)), ((), ())), preferred_element_type=F32)


def fold(a):
    return jnp.concatenate([a[:, :, :128], a[:, :, 128:]], axis=1)


def unfold(a):
    half = a.shape[1] // 2
    return jnp.concatenate([a[:, :half], a[:, half:]], axis=2)


def outward(n, i):
    return n // 2 + (1 - 2 * (i % 2)) * ((i + 1) // 2)


def split(a):
    high = a.astype(BF16)
    return high, (a - high.astype(F32)).astype(BF16)


def kernel(
    n_graph, n_feat,
    feat_hbm, w1_hbm, w2_hbm, cot_hbm, near1_hbm, send_hbm, near2_hbm,
    out_ref, g2_ref, g1_ref,
    feat_ref, near1_ref, w2_ref, cot_ref, send_ref, near2_ref,
    table, x_own, x_all, w_all, pre_own, pre_out, pre_in, d_all, hid_own, hid_in,
    v_out, v_in, e_out, e_in, hh_out, hh_in,
    gs_out, gs_in, gz, gz_in, gfin, gsib, dw_out, dw_in, dz, dz_in,
    send_sem, recv_sem, load_sem,
):
    n_chip = n_feat // 2
    n_y = n_chip // N_X
    n_block = 2 * N_X
    rows_x = 2 * n_y * OWN
    n_tiles = min(2, N_X)
    tile = N_X * rows_x // n_tiles
    shard = HID // n_chip
    g = lax.axis_index("graph")
    f = lax.axis_index("feat")
    chip, core = f // 2, f % 2
    x, y = chip // n_y, chip % n_y
    sibling = f + 1 - 2 * core
    block_own = 2 * x + core
    sheet = x * n_y + (1 - core) * y + core * g

    depth = (1 - core) * y + core * g
    around = (1 - core) * g + core * y
    turn_x = [(x + outward(N_X, i)) % N_X for i in range(N_X)]
    turn_d = [(depth + outward(n_y, i)) % n_y for i in range(n_y)]
    turn_a = [(around + outward(n_y, i)) % n_y for i in range(n_y)]
    graphs = [(g + outward(n_graph, i)) % n_graph for i in range(n_graph - 1)]
    sheet_x = [2 * n_y * to + core for to in turn_x]
    sheet_f = [2 * ((1 - core) * to + core * y) for to in turn_d]
    sheet_g = [(1 - core) * g + core * to for to in turn_d]
    sheet_peers = [
        (turn_x[i % N_X] * n_y + turn_d[i // N_X], sheet_g[i // N_X], sheet_x[i % N_X] + sheet_f[i // N_X])
        for i in range(n_chip - 1)
    ]
    ring_peers = [
        ((1 - core) * to + core * g, 2 * (x * n_y + (1 - core) * y + core * to) + core) for to in turn_a[:-1]
    ]
    block_peers = [
        (2 * to + other, 2 * (to * n_y + y) + other) for to in turn_x for other in (1 - core, core)
    ][:-1]
    column = [(y + outward(n_y, i)) % n_y for i in range(n_y - 1)]
    column_peers = [(to, 2 * (x * n_y + to) + core) for to in column]
    column_sources = [2 * (x * n_y + (y - outward(n_y, i) + n_y) % n_y) + core for i in range(n_y - 1)]

    def remote(index, src, dst, graph, feat):
        return pltpu.make_async_remote_copy(
            src_ref=src, dst_ref=dst, send_sem=send_sem.at[index], recv_sem=recv_sem.at[index],
            device_id=(graph, feat), device_id_type=MESH,
        )

    def wait_in(index, ref):
        remote(index, ref, ref, g, sibling).wait_recv()

    def wait_out(index, ref):
        remote(index, ref, ref, g, sibling).wait_send()

    loads = [
        pltpu.make_async_copy(src, dst, load_sem.at[i])
        for i, (src, dst) in enumerate((
            (feat_hbm, feat_ref), (near1_hbm, near1_ref), (w1_hbm, w_all.at[n_y - 1]), (cot_hbm, cot_ref),
            (near2_hbm, near2_ref), (send_hbm, send_ref), (w2_hbm, w2_ref),
        ))
    ]
    for load in loads:
        load.start()

    barrier = pltpu.get_barrier_semaphore()

    def greet(graph, feat):
        pl.semaphore_signal(barrier, inc=1, device_id=(graph, feat), device_id_type=MESH)

    for _, graph, feat in sheet_peers:
        greet(graph, feat)
    for graph, feat in ring_peers:
        greet(graph, feat)

    for i in range(0, n_block, 2):
        greet(g, block_peers[i][1])

    loads[0].wait()
    loads[1].wait()
    for s in range(GROUPS):
        table[s * 8 : (s + 1) * 8, :] = feat_ref[:, s * LO : (s + 1) * LO].astype(F32)
    lows = lax.broadcasted_iota(jnp.int32, (LO, tile), 0).astype(F32).astype(BF16)

    def gather(t):
        columns = pl.ds(pl.multiple_of(t * tile, tile), tile)
        near = near1_ref[:, columns]
        groups = table[...].astype(BF16)
        total = jnp.zeros((8, tile), F32)
        for k in range(FAN1):
            index = near[k : k + 1]
            low = jnp.broadcast_to((index % LO).astype(F32), (16, tile)).astype(BF16)
            low = jnp.concatenate([low] * (LO // 16), axis=0)
            picked = dot(groups, jnp.where(lows == low, jnp.ones((), BF16), jnp.zeros((), BF16)))
            high = jnp.broadcast_to(index // LO, (8, tile))
            masks = [(high // (1 << bit)) % 2 != 0 for bit in range(4)]
            total = total + select_tree([picked[s * 8 : (s + 1) * 8] for s in range(GROUPS)], masks)
        both = jnp.concatenate([feat_ref[:, columns].astype(F32), total / FAN1], axis=0).astype(BF16)
        for k in range(n_y):
            starts = [i * rows_x + 2 * k * OWN for i in range(tile // rows_x)]
            x_own[t, k] = jnp.concatenate([both[:, j : j + 2 * OWN] for j in starts], axis=1)

    def step(t, carry):
        gather(t)

        @pl.when(t == 0)
        def _():
            pl.semaphore_wait(barrier, n_chip - 1 + n_graph - 1 + N_X)
            loads[2].wait()
            own = w_all.at[n_y - 1]
            for i, (_, feat) in enumerate(column_peers):
                remote(0, own, w_all.at[i], g, feat).start()

        for i, (to, feat) in enumerate(column_peers):
            remote(14 + t, x_own.at[t, to], x_all.at[t, i], g, feat).start()
        x_all[t, n_y - 1] = x_own[t, y]
        return carry

    lax.fori_loop(0, n_tiles, step, 0)

    loads[3].wait()
    loads[4].wait()
    width = OWN + n_graph * HALO
    near2 = near2_ref[...]
    slots = lax.broadcasted_iota(jnp.int32, (width, OWN), 0)
    counts_t = jnp.zeros((width, OWN), F32)
    for k in range(FAN2):
        counts_t = counts_t + jnp.where(slots == near2[k : k + 1], 1.0, 0.0)
    counts_t = counts_t.astype(BF16)
    cot = cot_ref[...]
    e_all = dot(counts_t, cot)
    e_out[...] = fold(e_all[OWN:].reshape(n_graph, HALO, HID)).astype(BF16)
    for peer in graphs:
        remote(2, e_out.at[peer], e_in.at[g], peer, f).start()
    loads[5].wait()
    loads[6].wait()
    rows = lax.broadcasted_iota(jnp.int32, (OWN, n_graph * HALO), 0)
    sent = send_ref[...]
    sent = jnp.concatenate([sent[p : p + 1] for p in range(n_graph)], axis=1)
    pick_t = jnp.where(rows == sent, 1.0, 0.0).astype(BF16)

    wait_in(0, w_all.at[pl.ds(0, n_y - 1)])
    owners = n_block // n_tiles
    weights = w_all[...].reshape(n_y * 16, HID)
    inputs = []
    for t in range(n_tiles):
        wait_in(14 + t, x_all.at[t, pl.ds(0, n_y - 1)])
        inputs.append(x_all[t].reshape(n_y * 16, owners * OWN))
        sums = dot_lhs_t(inputs[t], weights).reshape(owners, OWN, HID)
        pre_own[t * owners : (t + 1) * owners] = sums
        pre_out[t * owners : (t + 1) * owners] = sums.astype(BF16)
        for i, (block, feat) in enumerate(block_peers):

            @pl.when(block // owners == t)
            def _(i=i, block=block, feat=feat):
                remote(4, pre_out.at[block], pre_in.at[i], g, feat).start()

    e_in[g] = jnp.zeros((2 * HALO, HID // 2), BF16)
    wait_in(2, e_in.at[pl.ds(0, n_graph - 1)])
    back = unfold(e_in[...].astype(F32)).reshape(n_graph * HALO, HID).astype(BF16)
    e_total = (e_all[:OWN] + dot(pick_t, back)) / FAN2
    e_high, e_low = split(e_total)
    first = jnp.broadcast_to(core, (OWN, HID)) == 0
    cot32, e32 = cot.astype(F32), e_high.astype(F32)
    v_own = jnp.where(first, cot32, e32).astype(BF16)
    v_out[...] = jnp.where(first, e32, cot32).astype(BF16)
    remote(3, v_out, v_in, g, sibling).start()
    d_hidden = dot_rhs_t(cot, w2_ref[0]) + (dot_rhs_t(e_high, w2_ref[1]) + dot_rhs_t(e_low, w2_ref[1]))

    wait_in(4, pre_in.at[pl.ds(0, n_block - 1)])
    pre = pre_own[block_own] + jnp.sum(pre_in[pl.ds(0, n_block - 1)].astype(F32), axis=0)
    sig = 1.0 / (1.0 + jnp.exp(-pre))
    hidden = (pre * sig).astype(BF16)
    hid_own[...] = hidden
    remote(5, hid_own, hid_in, g, sibling).start()
    d_all[block_own] = (d_hidden * (sig * (1.0 + pre * (1.0 - sig)))).astype(BF16)
    hh_out[...] = fold(dot_lhs_t(pick_t, hidden).reshape(n_graph, HALO, HID)).astype(BF16)

    wait_in(3, v_in)
    v_pair = jnp.concatenate([v_own, v_in[...]], axis=0)
    wait_in(5, hid_in)
    grad = dot_lhs_t(jnp.concatenate([hidden, hid_in[...]], axis=0), v_pair).reshape(n_chip, shard, HID)
    gs_out[...] = fold(grad).astype(BF16)

    for i, (peer, graph, feat) in enumerate(sheet_peers):
        remote(8, gs_out.at[peer], gs_in.at[i], graph, feat).start()
    gs_in[n_chip - 1] = gs_out[sheet]

    for _, feat in block_peers:
        remote(6, d_all.at[block_own], d_all.at[block_own], g, feat).start()
    for peer in graphs:
        remote(7, hh_out.at[peer], hh_in.at[g], peer, f).start()

    wait_in(8, gs_in.at[pl.ds(0, n_chip - 1)])
    gz[...] = jnp.sum(gs_in[...].astype(F32), axis=0)
    for graph, feat in ring_peers:
        remote(10, gz, gz_in.at[around], graph, feat).start()
    gz_in[around] = gz[...]

    wait_in(6, d_all.at[pl.ds(0, n_block - 1)])
    grad_rows = d_all[...].reshape(n_tiles, owners * OWN, HID)
    dw = sum(dot(inputs[t], grad_rows[t]) for t in range(n_tiles))
    dw_out[...] = dw.reshape(n_y, 16, HID).astype(BF16)
    for i, feat in enumerate(column_sources):
        remote(9, dw_out.at[i], dw_in.at[i], g, feat).start()
    dw_in[n_y - 1] = dw_out[n_y - 1]

    wait_in(10, gz_in.at[pl.ds(0, n_graph - 1)])
    gfin[sheet] = jnp.sum(gz_in[...], axis=0).astype(BF16)
    for _, graph, feat in sheet_peers:
        remote(11, gfin.at[sheet], gfin.at[sheet], graph, feat).start()

    wait_in(9, dw_in.at[pl.ds(0, n_y - 1)])
    dz[...] = jnp.sum(dw_in[...].astype(F32), axis=0).astype(BF16)
    for peer in graphs:
        remote(12, dz, dz_in.at[g], peer, f).start()
    dz_in[g] = dz[...]

    hh_in[g] = jnp.zeros((2 * HALO, HID // 2), BF16)
    wait_in(7, hh_in.at[pl.ds(0, n_graph - 1)])
    halo = unfold(hh_in[...].astype(F32)).reshape(n_graph * HALO, HID)
    ext = jnp.concatenate([hidden.astype(F32), halo], axis=0).astype(BF16)
    mean2 = (dot_lhs_t(counts_t, ext) / FAN2).astype(BF16)
    out_ref[...] = (dot(hidden, w2_ref[0]) + dot(mean2, w2_ref[1])).astype(BF16)

    def unpack(ref, which):
        both = ref[...].astype(F32)
        g2_ref[which, :, 0:128] = both[:, :shard].reshape(HID, 128)
        g2_ref[which, :, 128:256] = both[:, shard:].reshape(HID, 128)

    wait_in(11, gfin.at[pl.ds(0, n_chip - 1)])
    remote(13, gfin, gsib, g, sibling).start()
    unpack(gfin, core)
    wait_in(12, dz_in.at[pl.ds(0, n_graph - 1)])
    g1_ref[...] = jnp.sum(dz_in[...].astype(F32), axis=0).reshape(2, 8, HID)
    wait_in(13, gsib)
    unpack(gsib, 1 - core)

    wait_out(0, w_all.at[pl.ds(0, n_y - 1)])
    for t in range(n_tiles):
        wait_out(14 + t, x_all.at[t, pl.ds(0, n_y - 1)])
    wait_out(2, e_in.at[pl.ds(0, n_graph - 1)])
    wait_out(3, v_in)
    wait_out(4, pre_in.at[pl.ds(0, n_block - 1)])
    wait_out(5, hid_in)
    wait_out(6, d_all.at[pl.ds(0, n_block - 1)])
    wait_out(7, hh_in.at[pl.ds(0, n_graph - 1)])
    wait_out(8, gs_in.at[pl.ds(0, n_chip - 1)])
    wait_out(9, dw_in.at[pl.ds(0, n_y - 1)])
    wait_out(10, gz_in.at[pl.ds(0, n_graph - 1)])
    wait_out(11, gfin.at[pl.ds(0, n_chip - 1)])
    wait_out(12, dz_in.at[pl.ds(0, n_graph - 1)])
    wait_out(13, gsib)


def store_kernel(a_ref, b_ref, c_ref, a_out, b_out, c_out, sem):
    copies = [
        pltpu.make_async_copy(src, dst, sem.at[i])
        for i, (src, dst) in enumerate(((b_ref, b_out), (a_ref, a_out), (c_ref, c_out)))
    ]
    for copy in copies:
        copy.start()
    for copy in copies:
        copy.wait()


def solution(mesh):
    n_graph, n_feat = mesh.shape["graph"], mesh.shape["feat"]
    n_chip, n_block = n_feat // 2, 2 * N_X
    n_y, n_tiles = n_chip // N_X, min(2, N_X)
    pack = 2 * HID // n_chip

    def body(features, w_first, w_second, cotangent, nbr_first, send_rows, nbr_second):
        vmem = pl.BlockSpec(memory_space=pltpu.VMEM)
        hbm = pl.BlockSpec(memory_space=pltpu.HBM)
        shapes = (
            jax.ShapeDtypeStruct((OWN, HID), BF16),
            jax.ShapeDtypeStruct((2, HID, HID), F32),
            jax.ShapeDtypeStruct((2, 8, HID), F32),
        )
        results = pl.pallas_call(
            functools.partial(kernel, n_graph, n_feat),
            out_shape=tuple(pltpu.VMEM(a.shape, a.dtype) for a in shapes),
            in_specs=[hbm] * 7,
            out_specs=(vmem,) * 3,
            scratch_shapes=[
                pltpu.VMEM((8, SRC), BF16),
                pltpu.VMEM((FAN1, n_feat * OWN), jnp.int32),
                pltpu.VMEM((2, HID, HID), BF16),
                pltpu.VMEM((OWN, HID), BF16),
                pltpu.VMEM((n_graph, HALO), jnp.int32),
                pltpu.VMEM((FAN2, OWN), jnp.int32),
                pltpu.VMEM((GROUPS * 8, LO), F32),
                pltpu.VMEM((n_tiles, n_y, 16, n_block // n_tiles * OWN), BF16),
                pltpu.VMEM((n_tiles, n_y, 16, n_block // n_tiles * OWN), BF16),
                pltpu.VMEM((n_y, 16, HID), BF16),
                pltpu.VMEM((n_block, OWN, HID), F32),
                pltpu.VMEM((n_block, OWN, HID), BF16),
                pltpu.VMEM((n_block, OWN, HID), BF16),
                pltpu.VMEM((n_block, OWN, HID), BF16),
                pltpu.VMEM((OWN, HID), BF16),
                pltpu.VMEM((OWN, HID), BF16),
                pltpu.VMEM((OWN, HID), BF16),
                pltpu.VMEM((OWN, HID), BF16),
                pltpu.VMEM((n_graph, 2 * HALO, HID // 2), BF16),
                pltpu.VMEM((n_graph, 2 * HALO, HID // 2), BF16),
                pltpu.VMEM((n_graph, 2 * HALO, HID // 2), BF16),
                pltpu.VMEM((n_graph, 2 * HALO, HID // 2), BF16),
                pltpu.VMEM((n_chip, pack, 128), BF16),
                pltpu.VMEM((n_chip, pack, 128), BF16),
                pltpu.VMEM((pack, 128), F32),
                pltpu.VMEM((n_graph, pack, 128), F32),
                pltpu.VMEM((n_chip, pack, 128), BF16),
                pltpu.VMEM((n_chip, pack, 128), BF16),
                pltpu.VMEM((n_y, 16, HID), BF16),
                pltpu.VMEM((n_y, 16, HID), BF16),
                pltpu.VMEM((16, HID), BF16),
                pltpu.VMEM((n_graph, 16, HID), BF16),
                pltpu.SemaphoreType.DMA((16,)),
                pltpu.SemaphoreType.DMA((16,)),
                pltpu.SemaphoreType.DMA((7,)),
            ],
            compiler_params=pltpu.CompilerParams(
                collective_id=0, has_side_effects=True, vmem_limit_bytes=40 * 1024 * 1024
            ),
        )(
            *(
                pltpu.with_memory_space_constraint(a, pltpu.HBM)
                for a in (
                    features.T,
                    w_first.reshape(16, HID),
                    w_second,
                    cotangent,
                    nbr_first.T,
                    send_rows.reshape(n_graph, HALO),
                    nbr_second.T,
                )
            )
        )
        return pl.pallas_call(
            store_kernel,
            out_shape=shapes,
            in_specs=[vmem] * 3,
            out_specs=(hbm,) * 3,
            scratch_shapes=[pltpu.SemaphoreType.DMA((3,))],
        )(*(pltpu.with_memory_space_constraint(a, pltpu.VMEM) for a in results))

    in_specs = (
        P("graph", "feat"),
        P(None, "feat", None),
        P(),
        P(("graph", "feat"), None),
        P("graph", None),
        P(("graph", "feat"), None, None),
        P(("graph", "feat"), None),
    )
    out_specs = (P(("graph", "feat"), None), P(), P(None, "feat", None))
    return jax.shard_map(body, mesh=mesh, in_specs=in_specs, out_specs=out_specs, check_vma=False)
```

time: 49.3 us -> 47.8 us (0.970)
  Pallas kernels: 48.6 us -> 47 us
    pallas_call x1, Pallas kernels: 47.7 us -> 46.2 us  [body(): pl.pallas_call(functools.partial(kernel, n_graph, n_feat), out_shape=tupl...]
where the time goes in v4:
time: 47.8 us; the launch traced here: 47.7 us
  Pallas kernels  47 us (98%)
  between operations  0.64 us (1%)
    pallas_call x1, Pallas kernels, body(): pl.pallas_call(functools.partial(kernel, n_graph, n_feat), out_shape=tupl...  46.2 us

profile of v4, /device:TPU:1, one launch (start us, length us, event | category | flops | bytes accessed | tf_op | source)
XLA Modules:
  0.0 47.7 jit_solution(9354963847852139814)
XLA Ops:
  0.6 46.2 %shard_map.94 = (bf16[32,256]{1,0:T(8,128)(2,1)S(1)}, f32[2,256,256]{2,1,0:T(8,128)S(1)}, f32[2,8,256]{2,1,0:T(8,128)S(1)}) custom-call(bf16[8,4096]{1,0:T(8,128)(2,1)} %bitcast.6, bf16[16,256]{1,0:T(8,128)(2,1)} %bitcast.7, bf16[2,256,256]{2,1,0:T(8,128)(2,1)} %w2_hbm.1, bf16[32,256]{1,0:T(8,128)(2,1)} %cot_hbm.1, s32[15,2048]{1,0:T(8,128)} %bitcast.5, ...), custom_call_target="tpu_custom_call" | custom-call | tf_op jit(solution)/shard_map/pallas_call | solution.py:347
  46.8 0.8 %shard_map.95 = (bf16[32,256]{1,0:T(8,128)(2,1)}, f32[2,256,256]{2,1,0:T(8,128)}, f32[2,8,256]{2,1,0:T(8,128)}) custom-call(bf16[32,256]{1,0:T(8,128)(2,1)S(1)} %get-tuple-element.6.a_ref, f32[2,256,256]{2,1,0:T(8,128)S(1)} %get-tuple-element.7.b_ref, f32[2,8,256]{2,1,0:T(8,128)S(1)} %get-tuple-element.8.c_ref), custom_call_target="tpu_custom_call" | custom-call | tf_op jit(solution)/shard_map/pallas_call | solution.py:406

commit v5 on v4

--- a/solution.py
+++ b/solution.py
@@ -64,7 +64,7 @@
     feat_hbm, w1_hbm, w2_hbm, cot_hbm, near1_hbm, send_hbm, near2_hbm,
     out_ref, g2_ref, g1_ref,
     feat_ref, near1_ref, w2_ref, cot_ref, send_ref, near2_ref,
-    table, x_own, x_all, w_all, pre_own, pre_out, pre_in, d_all, hid_own, hid_in,
+    table, x_own, x_all, w_all, pre_own, pre_out, pre_in, d_all,
     v_out, v_in, e_out, e_in, hh_out, hh_in,
     gs_out, gs_in, gz, gz_in, gfin, gsib, dw_out, dw_in, dz, dz_in,
     send_sem, recv_sem, load_sem,
@@ -219,7 +219,7 @@
 
             @pl.when(block // owners == t)
             def _(i=i, block=block, feat=feat):
-                remote(4, pre_out.at[block], pre_in.at[i], g, feat).start()
+                remote(4, pre_out.at[pl.ds(block // 2 * 2, 2)], pre_in.at[pl.ds(2 * i, 2)], g, feat).start()
 
     e_in[g] = jnp.zeros((2 * HALO, HID // 2), BF16)
     wait_in(2, e_in.at[pl.ds(0, n_graph - 1)])
@@ -233,19 +233,20 @@
     remote(3, v_out, v_in, g, sibling).start()
     d_hidden = dot_rhs_t(cot, w2_ref[0]) + (dot_rhs_t(e_high, w2_ref[1]) + dot_rhs_t(e_low, w2_ref[1]))
 
-    wait_in(4, pre_in.at[pl.ds(0, n_block - 1)])
-    pre = pre_own[block_own] + jnp.sum(pre_in[pl.ds(0, n_block - 1)].astype(F32), axis=0)
+    wait_in(4, pre_in.at[pl.ds(0, 2 * n_block - 2)])
+    pair = (n_block - 1, 2, OWN, HID)
+    pre_both = pre_own[pl.ds(2 * x, 2)] + jnp.sum(pre_in[pl.ds(0, 2 * n_block - 2)].astype(F32).reshape(pair), axis=0)
+    hid_both = (pre_both * (1.0 / (1.0 + jnp.exp(-pre_both)))).astype(BF16)
+    pre = jnp.where(first, pre_both[0], pre_both[1])
     sig = 1.0 / (1.0 + jnp.exp(-pre))
     hidden = (pre * sig).astype(BF16)
-    hid_own[...] = hidden
-    remote(5, hid_own, hid_in, g, sibling).start()
     d_all[block_own] = (d_hidden * (sig * (1.0 + pre * (1.0 - sig)))).astype(BF16)
     hh_out[...] = fold(dot_lhs_t(pick_t, hidden).reshape(n_graph, HALO, HID)).astype(BF16)
 
     wait_in(3, v_in)
-    v_pair = jnp.concatenate([v_own, v_in[...]], axis=0)
-    wait_in(5, hid_in)
-    grad = dot_lhs_t(jnp.concatenate([hidden, hid_in[...]], axis=0), v_pair).reshape(n_chip, shard, HID)
+    v_own32, v_in32 = v_own.astype(F32), v_in[...].astype(F32)
+    v_pair = jnp.concatenate([jnp.where(first, v_own32, v_in32), jnp.where(first, v_in32, v_own32)], axis=0).astype(BF16)
+    grad = dot_lhs_t(hid_both.reshape(2 * OWN, HID), v_pair).reshape(n_chip, shard, HID)
     gs_out[...] = fold(grad).astype(BF16)
 
     for i, (peer, graph, feat) in enumerate(sheet_peers):
@@ -307,8 +308,7 @@
         wait_out(14 + t, x_all.at[t, pl.ds(0, n_y - 1)])
     wait_out(2, e_in.at[pl.ds(0, n_graph - 1)])
     wait_out(3, v_in)
-    wait_out(4, pre_in.at[pl.ds(0, n_block - 1)])
-    wait_out(5, hid_in)
+    wait_out(4, pre_in.at[pl.ds(0, 2 * n_block - 2)])
     wait_out(6, d_all.at[pl.ds(0, n_block - 1)])
     wait_out(7, hh_in.at[pl.ds(0, n_graph - 1)])
     wait_out(8, gs_in.at[pl.ds(0, n_chip - 1)])
@@ -362,10 +362,8 @@
                 pltpu.VMEM((n_y, 16, HID), BF16),
                 pltpu.VMEM((n_block, OWN, HID), F32),
                 pltpu.VMEM((n_block, OWN, HID), BF16),
+                pltpu.VMEM((2 * n_block, OWN, HID), BF16),
                 pltpu.VMEM((n_block, OWN, HID), BF16),
-                pltpu.VMEM((n_block, OWN, HID), BF16),
-                pltpu.VMEM((OWN, HID), BF16),
-                pltpu.VMEM((OWN, HID), BF16),
                 pltpu.VMEM((OWN, HID), BF16),
                 pltpu.VMEM((OWN, HID), BF16),
                 pltpu.VMEM((n_graph, 2 * HALO, HID // 2), BF16),

time: 47.8 us -> 50.1 us (1.048)
  Pallas kernels: 47 us -> 49.3 us
    pallas_call x1, Pallas kernels: 46.2 us -> 48.5 us  [body(): pl.pallas_call(functools.partial(kernel, n_graph, n_feat), out_shape=tupl...]
where the time goes in v5:
time: 50.1 us; the launch traced here: 49.9 us
  Pallas kernels  49.3 us (98%)
  between operations  0.64 us (1%)
    pallas_call x1, Pallas kernels, body(): pl.pallas_call(functools.partial(kernel, n_graph, n_feat), out_shape=tupl...  48.5 us

profile of v5, /device:TPU:1, one launch (start us, length us, event | category | flops | bytes accessed | tf_op | source)
XLA Modules:
  0.0 49.9 jit_solution(11264927052308822617)
XLA Ops:
  0.6 48.5 %shard_map.94 = (bf16[32,256]{1,0:T(8,128)(2,1)S(1)}, f32[2,256,256]{2,1,0:T(8,128)S(1)}, f32[2,8,256]{2,1,0:T(8,128)S(1)}) custom-call(bf16[8,4096]{1,0:T(8,128)(2,1)} %bitcast.6, bf16[16,256]{1,0:T(8,128)(2,1)} %bitcast.7, bf16[2,256,256]{2,1,0:T(8,128)(2,1)} %w2_hbm.1, bf16[32,256]{1,0:T(8,128)(2,1)} %cot_hbm.1, s32[15,2048]{1,0:T(8,128)} %bitcast.5, ...), custom_call_target="tpu_custom_call" | custom-call | tf_op jit(solution)/shard_map/pallas_call | solution.py:347
  49.1 0.8 %shard_map.95 = (bf16[32,256]{1,0:T(8,128)(2,1)}, f32[2,256,256]{2,1,0:T(8,128)}, f32[2,8,256]{2,1,0:T(8,128)}) custom-call(bf16[32,256]{1,0:T(8,128)(2,1)S(1)} %get-tuple-element.6.a_ref, f32[2,256,256]{2,1,0:T(8,128)S(1)} %get-tuple-element.7.b_ref, f32[2,8,256]{2,1,0:T(8,128)S(1)} %get-tuple-element.8.c_ref), custom_call_target="tpu_custom_call" | custom-call | tf_op jit(solution)/shard_map/pallas_call | solution.py:404

commit v6 on v4

--- a/solution.py
+++ b/solution.py
@@ -299,9 +299,6 @@
     unpack(gfin, core)
     wait_in(12, dz_in.at[pl.ds(0, n_graph - 1)])
     g1_ref[...] = jnp.sum(dz_in[...].astype(F32), axis=0).reshape(2, 8, HID)
-    wait_in(13, gsib)
-    unpack(gsib, 1 - core)
-
     wait_out(0, w_all.at[pl.ds(0, n_y - 1)])
     for t in range(n_tiles):
         wait_out(14 + t, x_all.at[t, pl.ds(0, n_y - 1)])
@@ -316,6 +313,9 @@
     wait_out(10, gz_in.at[pl.ds(0, n_graph - 1)])
     wait_out(11, gfin.at[pl.ds(0, n_chip - 1)])
     wait_out(12, dz_in.at[pl.ds(0, n_graph - 1)])
+    wait_in(13, gsib)
+    unpack(gsib, 1 - core)
+
     wait_out(13, gsib)
 
 

time: 47.8 us -> 47.8 us (level)
  no operation moved by 1% of the time
where the time goes in v6:
time: 47.8 us; the launch traced here: 47.6 us
  Pallas kernels  47 us (98%)
  between operations  0.64 us (1%)
    pallas_call x1, Pallas kernels, body(): pl.pallas_call(functools.partial(kernel, n_graph, n_feat), out_shape=tupl...  46.2 us

profile of v6, /device:TPU:1, one launch (start us, length us, event | category | flops | bytes accessed | tf_op | source)
XLA Modules:
  0.0 47.6 jit_solution(13221294824627072043)
XLA Ops:
  0.6 46.2 %shard_map.94 = (bf16[32,256]{1,0:T(8,128)(2,1)S(1)}, f32[2,256,256]{2,1,0:T(8,128)S(1)}, f32[2,8,256]{2,1,0:T(8,128)S(1)}) custom-call(bf16[8,4096]{1,0:T(8,128)(2,1)} %bitcast.6, bf16[16,256]{1,0:T(8,128)(2,1)} %bitcast.7, bf16[2,256,256]{2,1,0:T(8,128)(2,1)} %w2_hbm.1, bf16[32,256]{1,0:T(8,128)(2,1)} %cot_hbm.1, s32[15,2048]{1,0:T(8,128)} %bitcast.5, ...), custom_call_target="tpu_custom_call" | custom-call | tf_op jit(solution)/shard_map/pallas_call | solution.py:347
  46.8 0.8 %shard_map.95 = (bf16[32,256]{1,0:T(8,128)(2,1)}, f32[2,256,256]{2,1,0:T(8,128)}, f32[2,8,256]{2,1,0:T(8,128)}) custom-call(bf16[32,256]{1,0:T(8,128)(2,1)S(1)} %get-tuple-element.6.a_ref, f32[2,256,256]{2,1,0:T(8,128)S(1)} %get-tuple-element.7.b_ref, f32[2,8,256]{2,1,0:T(8,128)S(1)} %get-tuple-element.8.c_ref), custom_call_target="tpu_custom_call" | custom-call | tf_op jit(solution)/shard_map/pallas_call | solution.py:406
